TPU v7x, 32 devices: a whole 2x2x4 slice. The times are simulated.
32 devices in a mesh: pipe: 2 (over core), seq: 4 (over z), fsdp: 4 (over y, x).
Axes of the slice: x: 2, y: 2, z: 4, core: 2. Of those that a mesh axis runs over, the one named last changes fastest.
Arguments:
- section_input: bfloat16 [8, 256, 768], P('fsdp', 'seq'), may hold values from -6 to 6
- timesteps: int32 [8], P('fsdp'), may hold values from 0 to 999
- labels: int32 [8], P('fsdp'), may hold values from 0 to 999
- time_table: bfloat16 [1000, 768], P(None, 'fsdp'), may hold values from -5 to 5
- label_table: bfloat16 [1000, 768], P(None, 'fsdp'), may hold values from -5 to 5
- w_ada: bfloat16 [2, 768, 4608], P('pipe', 'fsdp'), may hold values from -0.21875 to 0.21875
- b_ada: bfloat16 [2, 4608], P('pipe', 'fsdp'), may hold values from -3 to 3
- w_qkv: bfloat16 [2, 768, 2304], P('pipe', 'fsdp'), may hold values from -0.21875 to 0.21875
- b_qv: bfloat16 [2, 1536], P('pipe', 'fsdp'), may hold values from -2 to 2
- w_out: bfloat16 [2, 768, 768], P('pipe', 'fsdp'), may hold values from -0.875 to 0.875
- b_out: bfloat16 [2, 768], P('pipe', 'fsdp'), may hold values from -2 to 2
- w_up: bfloat16 [2, 768, 3072], P('pipe', 'fsdp'), may hold values from -0.21875 to 0.21875
- b_up: bfloat16 [2, 3072], P('pipe', 'fsdp'), may hold values from -2 to 2
- w_down: bfloat16 [2, 3072, 768], P('pipe', 'fsdp'), may hold values from -0.15625 to 0.15625
- b_down: bfloat16 [2, 768], P('pipe', 'fsdp'), may hold values from -2 to 2
- out_grad: bfloat16 [8, 256, 768], P('fsdp', 'seq'), may hold values from -6 to 6
Outputs:
- section_out: bfloat16 [2, 8, 256, 768], P('pipe', 'fsdp', 'seq')
- section_in_grad: bfloat16 [2, 8, 256, 768], P('pipe', 'fsdp', 'seq')
- grad_time_table: float32 [1000, 768], P(None, 'fsdp')
- grad_label_table: float32 [1000, 768], P(None, 'fsdp')
- grad_w_ada: float32 [2, 768, 4608], P('pipe', 'fsdp')
- grad_b_ada: float32 [2, 4608], P('pipe', 'fsdp')
- grad_w_qkv: float32 [2, 768, 2304], P('pipe', 'fsdp')
- grad_b_qv: float32 [2, 1536], P('pipe', 'fsdp')
- grad_w_out: float32 [2, 768, 768], P('pipe', 'fsdp')
- grad_b_out: float32 [2, 768], P('pipe', 'fsdp')
- grad_w_up: float32 [2, 768, 3072], P('pipe', 'fsdp')
- grad_b_up: float32 [2, 3072], P('pipe', 'fsdp')
- grad_w_down: float32 [2, 3072, 768], P('pipe', 'fsdp')
- grad_b_down: float32 [2, 768], P('pipe', 'fsdp')
All inputs are finite; a program needn't handle non-finite values.
Results may differ from a plain program's by a relative error of at most 0.02.
The roundings to bfloat16 on the way count: a program that leaves them out, or rounds other values in their place, can miss the bound.
Values may be sent and summed in bfloat16 or wider, within the bound.
A program may use at most 192 MiB of HBM per device.

v0:
```python
import jax
import jax.numpy as jnp
from jax import lax
from jax.sharding import PartitionSpec as P

HEADS = 12
MICRO = 2


def passed_along(x, axis, by):
    count = lax.axis_size(axis)
    pairs = [(i, i + by) for i in range(count) if 0 <= i + by < count]
    return lax.ppermute(x, axis, pairs)


def for_sending(x):

    def short(part):
        return part.astype(jnp.bfloat16) if part.dtype == jnp.float32 else part

    return jax.tree.map(short, x)


def matmul(left, right):
    return lax.dot_general(
        left, right, (((left.ndim - 1,), (0,)), ((), ())), preferred_element_type=jnp.float32
    )


def against(left, right):
    return lax.dot_general(
        left, right, (((left.ndim - 1,), (1,)), ((), ())), preferred_element_type=jnp.float32
    )


def inner_rows(left, right):
    return lax.dot_general(
        left, right, (((0,), (0,)), ((), ())), preferred_element_type=jnp.float32
    )


def norm_parts(field):
    center = field - jnp.mean(field, axis=-1, keepdims=True)
    inverse = lax.rsqrt(jnp.mean(center * center, axis=-1, keepdims=True) + 1e-06)
    return (center * inverse, inverse)


def norm_back(normed, inverse, upstream):
    return inverse * (
        upstream
        - jnp.mean(upstream, axis=-1, keepdims=True)
        - normed * jnp.mean(upstream * normed, axis=-1, keepdims=True)
    )


def smooth_gate(value):
    return jax.nn.gelu(value, approximate=True)


def store(buffer, item, place, valid):
    current = lax.dynamic_index_in_dim(buffer, place, 0, keepdims=False)
    return lax.dynamic_update_index_in_dim(buffer, jnp.where(valid, item, current), place, 0)


def fetch(buffer, place):
    return lax.dynamic_index_in_dim(buffer, place, 0, keepdims=False)


def attend_forward(joined, factor):
    queries = joined[:, :, 0]
    key_rows = joined[:, :, 1]
    values = joined[:, :, 2]
    scores = (
        jnp.einsum("bqhd,bkhd->bhqk", queries, key_rows, preferred_element_type=jnp.float32)
        * factor
    )
    summit = jnp.max(scores, axis=-1, keepdims=True)
    raised = jnp.exp(scores - summit)
    total = jnp.sum(raised, axis=-1, keepdims=True)
    probs = (raised / total).astype(jnp.bfloat16)
    attended = jnp.einsum("bhqk,bkhd->bqhd", probs, values, preferred_element_type=jnp.float32)
    return (attended.astype(jnp.bfloat16), (summit + jnp.log(total))[..., 0])


def attend_backward(joined, log_total, d_attended, factor):
    queries = joined[:, :, 0]
    key_rows = joined[:, :, 1]
    values = joined[:, :, 2]
    scores = (
        jnp.einsum("bqhd,bkhd->bhqk", queries, key_rows, preferred_element_type=jnp.float32)
        * factor
    )
    probs = jnp.exp(scores - log_total[..., None])
    d_probs = jnp.einsum("bqhd,bkhd->bhqk", d_attended, values, preferred_element_type=jnp.float32)
    delta = jnp.sum(probs * d_probs, axis=-1, keepdims=True)
    d_scores = (probs * (d_probs - delta)).astype(jnp.bfloat16)
    d_queries = (
        jnp.einsum("bhqk,bkhd->bqhd", d_scores, key_rows, preferred_element_type=jnp.float32)
        * factor
    )
    d_keys = (
        jnp.einsum("bhqk,bqhd->bkhd", d_scores, queries, preferred_element_type=jnp.float32)
        * factor
    )
    d_values = jnp.einsum(
        "bhqk,bqhd->bkhd",
        probs.astype(jnp.bfloat16),
        d_attended,
        preferred_element_type=jnp.float32,
    )
    return jnp.stack([d_queries, d_keys, d_values], axis=2).astype(jnp.bfloat16)


def local(
    section_input,
    timesteps,
    labels,
    time_table,
    label_table,
    w_ada,
    b_ada,
    w_qkv,
    b_qv,
    w_out,
    b_out,
    w_up,
    b_up,
    w_down,
    b_down,
    out_grad,
):
    gathered = (
        lax.all_gather(time_table, "fsdp", axis=1, tiled=True),
        lax.all_gather(label_table, "fsdp", axis=1, tiled=True),
        lax.all_gather(w_ada, "fsdp", axis=1, tiled=True),
        lax.all_gather(b_ada, "fsdp", axis=1, tiled=True),
        lax.all_gather(w_qkv, "fsdp", axis=1, tiled=True),
        lax.all_gather(b_qv, "fsdp", axis=1, tiled=True),
        lax.all_gather(w_out, "fsdp", axis=1, tiled=True),
        lax.all_gather(b_out, "fsdp", axis=1, tiled=True),
        lax.all_gather(w_up, "fsdp", axis=1, tiled=True),
        lax.all_gather(b_up, "fsdp", axis=1, tiled=True),
        lax.all_gather(w_down, "fsdp", axis=1, tiled=True),
        lax.all_gather(b_down, "fsdp", axis=1, tiled=True),
    )
    time_full = gathered[0]
    label_full = gathered[1]
    weight_set = gathered[2:]
    time_hot = (timesteps[:, None] == jnp.arange(time_full.shape[0])[None, :]).astype(jnp.bfloat16)
    label_hot = (labels[:, None] == jnp.arange(label_full.shape[0])[None, :]).astype(jnp.bfloat16)
    cond = matmul(time_hot, time_full) + matmul(label_hot, label_full)
    (
        ada_weight,
        ada_bias,
        joined_weight,
        joined_bias,
        out_weight,
        out_bias,
        up_weight,
        up_bias,
        down_weight,
        down_bias,
    ) = tuple((item[0] for item in weight_set))
    section = lax.axis_index("pipe")
    seq_rank = lax.axis_index("seq")
    seq_count = lax.axis_size("seq")
    lat_dev, seq_dev, width = section_input.shape
    micro = MICRO
    group_lat = lat_dev // micro
    local_heads = HEADS // seq_count
    head_size = width // HEADS
    factor = head_size ** (-0.5)
    full_seq = seq_dev * seq_count
    hidden_width = up_weight.shape[1]
    scaled = jax.nn.silu(cond).astype(jnp.bfloat16)
    modulation = matmul(scaled, ada_weight) + ada_bias.astype(jnp.float32)
    bias_qkv = jnp.concatenate(
        [joined_bias[:width], jnp.zeros((width,), jnp.bfloat16), joined_bias[width:]]
    ).astype(jnp.float32)

    def section_forward(field, mods):
        parts = jnp.split(mods, 6, axis=-1)
        normed, _ = norm_parts(field)
        first_in = (normed * (1.0 + parts[1][:, None]) + parts[0][:, None]).astype(jnp.bfloat16)
        joined = (matmul(first_in, joined_weight) + bias_qkv).astype(jnp.bfloat16)
        joined = joined.reshape(group_lat, seq_dev, 3, HEADS, head_size)
        heads_joined = lax.all_to_all(joined, "seq", split_axis=3, concat_axis=1, tiled=True)
        attended, log_total = attend_forward(heads_joined, factor)
        back = lax.all_to_all(attended, "seq", split_axis=1, concat_axis=2, tiled=True).reshape(
            group_lat, seq_dev, width
        )
        branch = matmul(back, out_weight) + out_bias.astype(jnp.float32)
        middle = field + parts[2][:, None] * branch
        normed_mid, _ = norm_parts(middle)
        second_in = (normed_mid * (1.0 + parts[4][:, None]) + parts[3][:, None]).astype(
            jnp.bfloat16
        )
        hidden = matmul(second_in, up_weight) + up_bias.astype(jnp.float32)
        active = smooth_gate(hidden).astype(jnp.bfloat16)
        result = matmul(active, down_weight) + down_bias.astype(jnp.float32)
        output = middle + parts[5][:, None] * result
        return (output, (heads_joined, log_total, back, middle, hidden, result, branch))

    def section_backward(upstream, field, kept, mods):
        heads_joined, log_total, back, middle, hidden, result, branch = kept
        parts = jnp.split(mods, 6, axis=-1)
        d_result = (parts[5][:, None] * upstream).astype(jnp.bfloat16)
        d_active = against(d_result, down_weight)
        _, gate_pull = jax.vjp(smooth_gate, hidden)
        d_hidden = gate_pull(d_active)[0].astype(jnp.bfloat16)
        normed_mid, inverse_mid = norm_parts(middle)
        d_second = against(d_hidden, up_weight)
        d_middle = upstream + norm_back(
            normed_mid, inverse_mid, d_second * (1.0 + parts[4][:, None])
        )
        d_branch = (parts[2][:, None] * d_middle).astype(jnp.bfloat16)
        d_back = against(d_branch, out_weight).astype(jnp.bfloat16)
        d_heads = lax.all_to_all(
            d_back.reshape(group_lat, seq_dev, HEADS, head_size),
            "seq",
            split_axis=2,
            concat_axis=1,
            tiled=True,
        )
        d_joined_heads = attend_backward(heads_joined, log_total, d_heads, factor)
        d_joined = lax.all_to_all(
            d_joined_heads, "seq", split_axis=1, concat_axis=3, tiled=True
        ).reshape(group_lat, seq_dev, 3 * width)
        normed, inverse = norm_parts(field)
        d_first = against(d_joined, joined_weight)
        d_field = d_middle + norm_back(normed, inverse, d_first * (1.0 + parts[1][:, None]))
        d_mods = jnp.concatenate(
            [
                jnp.sum(d_first, axis=1),
                jnp.sum(d_first * normed, axis=1),
                jnp.sum(d_middle * branch, axis=1),
                jnp.sum(d_second, axis=1),
                jnp.sum(d_second * normed_mid, axis=1),
                jnp.sum(upstream * result, axis=1),
            ],
            axis=-1,
        )
        return (d_field, d_mods, (d_joined, d_branch, d_hidden, d_result))

    token_shape = (group_lat, seq_dev, width)
    inputs = section_input.reshape((micro,) + token_shape)
    upstreams = out_grad.reshape((micro,) + token_shape)
    keep_field = jnp.zeros((micro,) + token_shape, jnp.bfloat16)
    keep_joined = jnp.zeros((micro, group_lat, full_seq, 3, local_heads, head_size), jnp.bfloat16)
    keep_total = jnp.zeros((micro, group_lat, local_heads, full_seq), jnp.float32)
    keep_back = jnp.zeros((micro,) + token_shape, jnp.bfloat16)
    keep_middle = jnp.zeros((micro,) + token_shape, jnp.float32)
    keep_hidden = jnp.zeros((micro, group_lat, seq_dev, hidden_width), jnp.float32)
    keep_result = jnp.zeros((micro,) + token_shape, jnp.float32)
    keep_branch = jnp.zeros((micro,) + token_shape, jnp.float32)
    out_buffer = jnp.zeros((micro,) + token_shape, jnp.bfloat16)
    received = jnp.zeros(token_shape, jnp.bfloat16)
    mods_all = modulation.reshape(micro, group_lat, 6 * width)
    for tick in range(micro + 1):
        index = tick - section
        valid = (index >= 0) & (index < micro)
        place = jnp.clip(index, 0, micro - 1)
        entering = jnp.where(section == 0, inputs[min(tick, micro - 1)], received)
        output, kept = section_forward(entering.astype(jnp.float32), fetch(mods_all, place))
        sent = output.astype(jnp.bfloat16)
        keep_field = store(keep_field, entering, place, valid)
        keep_joined = store(keep_joined, kept[0], place, valid)
        keep_total = store(keep_total, kept[1], place, valid)
        keep_back = store(keep_back, kept[2], place, valid)
        keep_middle = store(keep_middle, kept[3], place, valid)
        keep_hidden = store(keep_hidden, kept[4], place, valid)
        keep_result = store(keep_result, kept[5], place, valid)
        keep_branch = store(keep_branch, kept[6], place, valid)
        out_buffer = store(out_buffer, sent, place, valid)
        if tick < micro:
            received = passed_along(sent, "pipe", 1)
    keep_d_joined = jnp.zeros((micro, group_lat, seq_dev, 3 * width), jnp.bfloat16)
    keep_d_branch = jnp.zeros((micro,) + token_shape, jnp.bfloat16)
    keep_d_hidden = jnp.zeros((micro, group_lat, seq_dev, hidden_width), jnp.bfloat16)
    keep_d_result = jnp.zeros((micro,) + token_shape, jnp.bfloat16)
    keep_d_mods = jnp.zeros((micro, group_lat, 6 * width), jnp.float32)
    grad_buffer = jnp.zeros((micro,) + token_shape, jnp.bfloat16)
    returned = jnp.zeros(token_shape, jnp.bfloat16)
    for tick in range(micro + 1):
        index = tick - (1 - section)
        valid = (index >= 0) & (index < micro)
        place = jnp.clip(index, 0, micro - 1)
        if tick < micro:
            own = upstreams[tick]
        else:
            own = jnp.zeros(token_shape, jnp.bfloat16)
        upstream = jnp.where(section == 1, own, returned).astype(jnp.float32)
        kept = (
            fetch(keep_joined, place),
            fetch(keep_total, place),
            fetch(keep_back, place),
            fetch(keep_middle, place),
            fetch(keep_hidden, place),
            fetch(keep_result, place),
            fetch(keep_branch, place),
        )
        field = fetch(keep_field, place).astype(jnp.float32)
        d_field, d_mods, d_parts = section_backward(upstream, field, kept, fetch(mods_all, place))
        sent_back = d_field.astype(jnp.bfloat16)
        grad_buffer = store(grad_buffer, sent_back, place, valid)
        keep_d_mods = store(keep_d_mods, d_mods, place, valid)
        keep_d_joined = store(keep_d_joined, d_parts[0], place, valid)
        keep_d_branch = store(keep_d_branch, d_parts[1], place, valid)
        keep_d_hidden = store(keep_d_hidden, d_parts[2], place, valid)
        keep_d_result = store(keep_d_result, d_parts[3], place, valid)
        if tick < micro:
            returned = passed_along(sent_back, "pipe", -1)
    rows = micro * group_lat * seq_dev
    parts_all = jnp.split(mods_all, 6, axis=-1)
    normed_all, _ = norm_parts(keep_field.astype(jnp.float32))
    first_all = (
        (normed_all * (1.0 + parts_all[1][:, :, None]) + parts_all[0][:, :, None])
        .astype(jnp.bfloat16)
        .reshape(rows, width)
    )
    normed_mid_all, _ = norm_parts(keep_middle)
    second_all = (
        (normed_mid_all * (1.0 + parts_all[4][:, :, None]) + parts_all[3][:, :, None])
        .astype(jnp.bfloat16)
        .reshape(rows, width)
    )
    active_all = smooth_gate(keep_hidden).astype(jnp.bfloat16).reshape(rows, hidden_width)
    d_joined_all = keep_d_joined.reshape(rows, 3 * width)
    d_branch_all = keep_d_branch.reshape(rows, width)
    d_hidden_all = keep_d_hidden.reshape(rows, hidden_width)
    d_result_all = keep_d_result.reshape(rows, width)
    grad_joined = inner_rows(first_all, d_joined_all)
    joined_sums = jnp.sum(d_joined_all, axis=0, dtype=jnp.float32)
    grad_qv = jnp.concatenate([joined_sums[:width], joined_sums[2 * width :]])
    grad_out = inner_rows(keep_back.reshape(rows, width), d_branch_all)
    grad_out_bias = jnp.sum(d_branch_all, axis=0, dtype=jnp.float32)
    grad_up = inner_rows(second_all, d_hidden_all)
    grad_up_bias = jnp.sum(d_hidden_all, axis=0, dtype=jnp.float32)
    grad_down = inner_rows(active_all, d_result_all)
    grad_down_bias = jnp.sum(d_result_all, axis=0, dtype=jnp.float32)
    d_mod_sum = lax.psum(keep_d_mods.reshape(lat_dev, 6 * width).astype(jnp.bfloat16), "seq")
    quarter = (jnp.arange(width) // (width // seq_count) == seq_rank).astype(jnp.float32)
    grad_ada = inner_rows(scaled, d_mod_sum) * quarter[:, None]
    grad_ada_bias = jnp.sum(d_mod_sum, axis=0, dtype=jnp.float32) * (seq_rank == 0).astype(
        jnp.float32
    )
    d_scaled = against(d_mod_sum, ada_weight)
    _, silu_pull = jax.vjp(jax.nn.silu, cond)
    d_cond = silu_pull(d_scaled)[0]
    d_cond = lax.psum(d_cond, "pipe")
    weight_partials = (
        grad_ada[None],
        grad_ada_bias[None],
        grad_joined[None],
        grad_qv[None],
        grad_out[None],
        grad_out_bias[None],
        grad_up[None],
        grad_up_bias[None],
        grad_down[None],
        grad_down_bias[None],
    )
    masked = d_cond * quarter[None, :]
    grad_time = lax.dot_general(
        time_hot.astype(jnp.float32),
        masked,
        (((0,), (0,)), ((), ())),
        precision=lax.Precision.HIGHEST,
    )
    grad_label = lax.dot_general(
        label_hot.astype(jnp.float32),
        masked,
        (((0,), (0,)), ((), ())),
        precision=lax.Precision.HIGHEST,
    )
    partials = (grad_time, grad_label) + weight_partials
    shards = jax.tree.map(
        lambda part: part.astype(jnp.float32),
        lax.psum_scatter(for_sending(partials), "fsdp", scatter_dimension=1, tiled=True),
    )
    shards = jax.tree.map(
        lambda part: part.astype(jnp.float32), lax.psum(for_sending(shards), "seq")
    )
    table_grads = (shards[0], shards[1])
    weight_grads = shards[2:]
    section_out = out_buffer.reshape((1, lat_dev, seq_dev, width))
    section_in_grad = grad_buffer.reshape((1, lat_dev, seq_dev, width))
    return (
        section_out,
        section_in_grad,
        table_grads[0],
        table_grads[1],
        weight_grads[0],
        weight_grads[1],
        weight_grads[2],
        weight_grads[3],
        weight_grads[4],
        weight_grads[5],
        weight_grads[6],
        weight_grads[7],
        weight_grads[8],
        weight_grads[9],
    )


def solution(mesh):
    in_specs = (
        P("fsdp", "seq", None),
        P("fsdp"),
        P("fsdp"),
        P(None, "fsdp"),
        P(None, "fsdp"),
        P("pipe", "fsdp", None),
        P("pipe", "fsdp"),
        P("pipe", "fsdp", None),
        P("pipe", "fsdp"),
        P("pipe", "fsdp", None),
        P("pipe", "fsdp"),
        P("pipe", "fsdp", None),
        P("pipe", "fsdp"),
        P("pipe", "fsdp", None),
        P("pipe", "fsdp"),
        P("fsdp", "seq", None),
    )
    out_specs = (
        P("pipe", "fsdp", "seq", None),
        P("pipe", "fsdp", "seq", None),
        P(None, "fsdp"),
        P(None, "fsdp"),
        P("pipe", "fsdp", None),
        P("pipe", "fsdp"),
        P("pipe", "fsdp", None),
        P("pipe", "fsdp"),
        P("pipe", "fsdp", None),
        P("pipe", "fsdp"),
        P("pipe", "fsdp", None),
        P("pipe", "fsdp"),
        P("pipe", "fsdp", None),
        P("pipe", "fsdp"),
    )
    return jax.shard_map(local, mesh=mesh, in_specs=in_specs, out_specs=out_specs, check_vma=False)
```

profile of v0, /device:TPU:0, one launch (start us, length us, event | category | flops | bytes accessed | tf_op | source)
XLA Modules:
  0.0 1446.8 jit_solution(10126765380043649996)
XLA Ops:
  13.8 11.4 all-reduce.2
  25.3 7.2 all_gather.45
  32.5 8.0 all_gather.41
  40.5 7.2 all_gather.39
  53.1 23.5 %all-gather.10.cloned.1.call-done = bf16[1000,768]{0,1:T(8,128)(2,1)} async-done(((bf16[1000,192]{0,1:T(8,128)(2,1)}), bf16[1000,768]{0,1:T(8,128)(2,1)}) %all-gather.10.cloned.1.call-update) | async-done | bytes 1536016 | tf_op jit(solution)/shard_map/all_gather | solution.py:134
  78.6 76.7 %all-gather.12.cloned.1.call-done = bf16[1,768,4608]{2,1,0:T(8,128)(2,1)} async-done(((bf16[1,192,4608]{2,1,0:T(8,128)(2,1)}), bf16[1,768,4608]{2,1,0:T(8,128)(2,1)}) %all-gather.12.cloned.1.call-update) | async-done | bytes 7077904 | tf_op jit(solution)/shard_map/all_gather | solution.py:135
  160.8 43.4 %all-gather.14.cloned.1.call-done = bf16[1,768,2304]{2,1,0:T(8,128)(2,1)} async-done(((bf16[1,192,2304]{2,1,0:T(8,128)(2,1)}), bf16[1,768,2304]{2,1,0:T(8,128)(2,1)}) %all-gather.14.cloned.1.call-update) | async-done | bytes 3538960 | tf_op jit(solution)/shard_map/all_gather | solution.py:137
  215.4 7.6 all-to-all-done
  241.5 51.0 %all-gather.18.cloned.1.call-done = bf16[1,768,3072]{2,1,0:T(8,128)(2,1)} async-done(((bf16[1,192,3072]{2,1,0:T(8,128)(2,1)}), bf16[1,768,3072]{2,1,0:T(8,128)(2,1)}) %all-gather.18.cloned.1.call-update) | async-done | bytes 4718608 | tf_op jit(solution)/shard_map/all_gather | solution.py:141
  298.2 53.2 %all-gather.20.cloned.1.call-done = bf16[1,3072,768]{2,1,0:T(8,128)(2,1)} async-done(((bf16[1,768,768]{2,1,0:T(8,128)(2,1)}), bf16[1,3072,768]{2,1,0:T(8,128)(2,1)}) %all-gather.20.cloned.1.call-update) | async-done | bytes 4718608 | tf_op jit(solution)/shard_map/all_gather | solution.py:143
  459.4 6.0 all-to-all-done.4
  721.6 17.6 %psum.98 = bf16[2,4608]{1,0:T(2,128)(2,1)S(1)} all-reduce(bf16[2,4608]{1,0:T(2,128)(2,1)} %dynamic_update_slice.176), channel_id=1, replica_groups=mesh['pipe'=2,'seq'=4,'fsdp'=4] {'seq'}, use_global_device_ids=true, to_apply=%region_63.64 | all-reduce | flops 9216 | bytes 36864 | tf_op jit(solution)/shard_map/psum | solution.py:341
  785.3 26.9 %reduce-scatter.23.cloned.1.call-done = bf16[1000,192]{0,1:T(8,128)(2,1)} async-done(((bf16[1000,768]{0,1:T(8,128)(2,1)}), bf16[1000,192]{0,1:T(8,128)(2,1)}) %reduce-scatter.23.cloned.1.call-update) | async-done | bytes 384016 | tf_op jit(solution)/shard_map/reduce_scatter | solution.py:379
  812.2 50.9 %reduce-scatter.29.cloned.1.call-done = bf16[1,192,2304]{2,1,0:T(8,128)(2,1)} async-done(((bf16[1,768,2304]{2,1,0:T(8,128)(2,1)}), bf16[1,192,2304]{2,1,0:T(8,128)(2,1)}) %reduce-scatter.29.cloned.1.call-update) | async-done | bytes 884752 | tf_op jit(solution)/shard_map/reduce_scatter | solution.py:379
  863.1 60.0 %reduce-scatter.35.cloned.1.call-done = bf16[1,768,768]{2,1,0:T(8,128)(2,1)} async-done(((bf16[1,3072,768]{2,1,0:T(8,128)(2,1)}), bf16[1,768,768]{2,1,0:T(8,128)(2,1)}) %reduce-scatter.35.cloned.1.call-update) | async-done | bytes 1179664 | tf_op jit(solution)/shard_map/reduce_scatter | solution.py:379
  923.1 60.1 %reduce-scatter.33.cloned.1.call-done = bf16[1,192,3072]{2,1,0:T(8,128)(2,1)} async-done(((bf16[1,768,3072]{2,1,0:T(8,128)(2,1)}), bf16[1,192,3072]{2,1,0:T(8,128)(2,1)}) %reduce-scatter.33.cloned.1.call-update) | async-done | bytes 1179664 | tf_op jit(solution)/shard_map/reduce_scatter | solution.py:379
  983.2 79.7 %reduce-scatter.27.cloned.1.call-done = bf16[1,192,4608]{2,1,0:T(8,128)(2,1)} async-done(((bf16[1,768,4608]{2,1,0:T(8,128)(2,1)}), bf16[1,192,4608]{2,1,0:T(8,128)(2,1)}) %reduce-scatter.27.cloned.1.call-update) | async-done | bytes 1769488 | tf_op jit(solution)/shard_map/reduce_scatter | solution.py:379
  1063.0 26.5 %reduce-scatter.45.cloned.1.call-done = bf16[192,1]{1,0:T(8,128)(2,1)} async-done(((bf16[768,1]{1,0:T(8,128)(2,1)}), bf16[192,1]{1,0:T(8,128)(2,1)}) %reduce-scatter.45.cloned.1.call-update) | async-done | bytes 400
  1090.4 25.7 %reduce-scatter.41.cloned.1.call-done = bf16[192,1]{1,0:T(8,128)(2,1)} async-done(((bf16[768,1]{1,0:T(8,128)(2,1)}), bf16[192,1]{1,0:T(8,128)(2,1)}) %reduce-scatter.41.cloned.1.call-update) | async-done | bytes 400
  1117.0 28.6 %reduce-scatter.43.cloned.1.call-done = bf16[768,1]{1,0:T(8,128)(2,1)} async-done(((bf16[3072,1]{1,0:T(8,128)(2,1)}), bf16[768,1]{1,0:T(8,128)(2,1)}) %reduce-scatter.43.cloned.1.call-update) | async-done | bytes 1552
  1147.7 25.5 %reduce-scatter.39.cloned.1.call-done = bf16[384,1]{1,0:T(8,128)(2,1)} async-done(((bf16[1536,1]{1,0:T(8,128)(2,1)}), bf16[384,1]{1,0:T(8,128)(2,1)}) %reduce-scatter.39.cloned.1.call-update) | async-done | bytes 784
  1174.2 31.1 %reduce-scatter.37.cloned.1.call-done = bf16[1152,1]{1,0:T(8,128)(2,1)} async-done(((bf16[4608,1]{1,0:T(8,128)(2,1)}), bf16[1152,1]{1,0:T(8,128)(2,1)}) %reduce-scatter.37.cloned.1.call-update) | async-done | bytes 2320
  1206.4 21.9 %all-reduce.3 = (bf16[1,1152]{1,0:T(2,128)(2,1)S(1)}, bf16[1,384]{1,0:T(2,128)(2,1)S(1)}, bf16[1,192]{1,0:T(2,128)(2,1)S(1)}, bf16[1,768]{1,0:T(2,128)(2,1)S(1)}, bf16[1,192]{1,0:T(2,128)(2,1)S(1)}) all-reduce(bf16[1,1152]{1,0:T(2,128)(2,1)S(1)} %copy.289, ...), channel_id=1, replica_groups=mesh['pipe'=2,'seq'=4,'fsdp'=4] {'seq'}, use_global_device_ids=true, to_apply=%region_73.74 | all-reduce | flops 2688 | bytes 10752 | tf_op jit(solution)/shard_map/psum | solution.py:382
  1231.1 195.7 %all-reduce.7.cloned.1.call-done = (bf16[1000,192]{0,1:T(8,128)(2,1)}, bf16[1000,192]{0,1:T(8,128)(2,1)}, bf16[1,192,4608]{2,1,0:T(8,128)(2,1)}, bf16[1,192,2304...) async-done(((bf16[1000,192]{0,1:T(8,128)(2,1)}, bf16[1000,192]{0,1:T(8,128)(2,1)}, ...) | async-done | bytes 6076432 | tf_op jit(solution)/shard_map/psum | solution.py:382
  (741 shorter events, 483.3 us)
Async XLA Ops:
  7.2 43.9 %all-gather.8.cloned.1.call-start = ((), (), s32[]{:S(2)}) async-start(), calls=%async_computation.24 | async-start | bytes 1966080 | tf_op jit(solution)/shard_map/all_gather | solution.py:133
  8.0 68.6 %all-gather.10.cloned.1.call-start = ((), (), s32[]{:S(2)}) async-start(), calls=%async_computation.25 | async-start | bytes 1966080 | tf_op jit(solution)/shard_map/all_gather | solution.py:134
  8.8 146.5 %all-gather.12.cloned.1.call-start = ((), (), s32[]{:S(2)}) async-start(), calls=%async_computation.26 | async-start | bytes 8847360 | tf_op jit(solution)/shard_map/all_gather | solution.py:135
  9.5 194.7 %all-gather.14.cloned.1.call-start = ((), (), s32[]{:S(2)}) async-start(), calls=%async_computation.27 | async-start | bytes 4423680 | tf_op jit(solution)/shard_map/all_gather | solution.py:137
  10.1 227.2 %all-gather.16.cloned.1.call-start = ((), (), s32[]{:S(2)}) async-start(), calls=%async_computation.28 | async-start | bytes 1474560 | tf_op jit(solution)/shard_map/all_gather | solution.py:139
  10.7 281.8 %all-gather.18.cloned.1.call-start = ((), (), s32[]{:S(2)}) async-start(), calls=%async_computation.29 | async-start | bytes 5898240 | tf_op jit(solution)/shard_map/all_gather | solution.py:141
  11.2 340.2 %all-gather.20.cloned.1.call-start = ((), (), s32[]{:S(2)}) async-start(), calls=%async_computation.30 | async-start | bytes 5898240 | tf_op jit(solution)/shard_map/all_gather | solution.py:143
  208.8 14.2 all-to-all-start
  370.5 13.8 all-to-all-start.2
  624.9 13.1 all-to-all-start.9
  693.7 13.8 all-to-all-start.11
  697.8 87.5 %reduce-scatter.31.cloned.1.call-start = ((), (), s32[]{:S(2)}) async-start(), calls=%async_computation.35 | async-start | bytes 1474560 | tf_op jit(solution)/shard_map/reduce_scatter | solution.py:379
  703.2 82.1 %reduce-scatter.25.cloned.1.call-start = ((), (), s32[]{:S(2)}) async-start(), calls=%async_computation.32 | async-start | bytes 1966080 | tf_op jit(solution)/shard_map/reduce_scatter | solution.py:379
  749.3 62.9 %reduce-scatter.23.cloned.1.call-start = ((), (), s32[]{:S(2)}) async-start(), calls=%async_computation.31 | async-start | bytes 1966080 | tf_op jit(solution)/shard_map/reduce_scatter | solution.py:379
  752.0 111.1 %reduce-scatter.29.cloned.1.call-start = ((), (), s32[]{:S(2)}) async-start(), calls=%async_computation.34 | async-start | bytes 4423680 | tf_op jit(solution)/shard_map/reduce_scatter | solution.py:379
  760.8 162.2 %reduce-scatter.35.cloned.1.call-start = ((), (), s32[]{:S(2)}) async-start(), calls=%async_computation.37 | async-start | bytes 5898240 | tf_op jit(solution)/shard_map/reduce_scatter | solution.py:379
  766.2 217.0 %reduce-scatter.33.cloned.1.call-start = ((), (), s32[]{:S(2)}) async-start(), calls=%async_computation.36 | async-start | bytes 5898240 | tf_op jit(solution)/shard_map/reduce_scatter | solution.py:379
  771.1 291.8 %reduce-scatter.27.cloned.1.call-start = ((), (), s32[]{:S(2)}) async-start(), calls=%async_computation.33 | async-start | bytes 8847360 | tf_op jit(solution)/shard_map/reduce_scatter | solution.py:379
  776.4 313.1 %reduce-scatter.45.cloned.1.call-start = ((), (), s32[]{:S(2)}) async-start(), calls=%async_computation.42 | async-start | bytes 245760
  778.3 337.9 %reduce-scatter.41.cloned.1.call-start = ((), (), s32[]{:S(2)}) async-start(), calls=%async_computation.40 | async-start | bytes 245760
  779.3 366.3 %reduce-scatter.43.cloned.1.call-start = ((), (), s32[]{:S(2)}) async-start(), calls=%async_computation.41 | async-start | bytes 983040
  780.7 392.5 %reduce-scatter.39.cloned.1.call-start = ((), (), s32[]{:S(2)}) async-start(), calls=%async_computation.39 | async-start | bytes 491520
  782.0 423.3 %reduce-scatter.37.cloned.1.call-start = ((), (), s32[]{:S(2)}) async-start(), calls=%async_computation.38 | async-start | bytes 1474560
  785.2 641.6 %all-reduce.7.cloned.1.call-start = ((), (), s32[]{:S(2)}) async-start(), calls=%async_computation.43 | async-start | bytes 12189696 | tf_op jit(solution)/shard_map/psum | solution.py:382
  (170 other events, 2992.9 us)
Sparse Core Ops, SparseCore 0:
  9.9 33.8 all-gather.7
  45.6 30.9 all-gather.9
  78.5 76.6 all-gather.11
  156.9 47.2 all-gather.13
  205.9 27.7 all-gather.15
  235.3 57.0 all-gather.17
  294.3 57.0 all-gather.19
  703.4 28.9 reduce-scatter.30
  749.4 28.3 reduce-scatter.24
  781.2 30.9 reduce-scatter.22
  815.8 47.2 reduce-scatter.28
  865.9 57.0 reduce-scatter.34
  926.1 57.0 reduce-scatter.32
  986.1 76.7 reduce-scatter.26
  1065.5 23.9 reduce-scatter.44
  1092.1 23.9 reduce-scatter.40
  1119.4 26.0 reduce-scatter.42
  1148.8 24.3 reduce-scatter.38
  1176.7 28.5 reduce-scatter.36
  1208.1 218.7 all-reduce.6
where the time goes:
time: 1460 us; the launch traced here: 1450 us
  waiting for transfers between devices  911 us (62%)
  local copies, waits for them, and re-layouts  197 us (13%)
  matrix products  127 us (9%)
  blocking collectives  75.9 us (5%)
  other arithmetic  60.5 us (4%)
  starting transfers between devices  57.2 us (4%)
  between operations  17.9 us (1%)
    reduce_scatter x7, waiting for transfers between devices, local(): lax.psum_scatter(for_sending(partials), 'fsdp', scatter_dimension=1, tile...  278 us
    psum x1, waiting for transfers between devices, local(): lax.psum(for_sending(shards), 'seq')  196 us
    unnamed x25, waiting for transfers between devices  142 us
    all_gather x1, waiting for transfers between devices, local(): lax.all_gather(w_ada, 'fsdp', axis=1, tiled=True)  76.7 us
    unnamed x371, local copies, waits for them, and re-layouts  73.7 us
    all_gather x1, waiting for transfers between devices, local(): lax.all_gather(w_down, 'fsdp', axis=1, tiled=True)  53.2 us
    all_gather x1, waiting for transfers between devices, local(): lax.all_gather(w_up, 'fsdp', axis=1, tiled=True)  51 us
    dot_general x15, matrix products, matmul(): lax.dot_general(left, right, (((left.ndim - 1,), (0,)), ((), ())), prefer...  45.9 us
  transfers between devices with their start and end apart: 36, of which 29 were waited for; matrix products, arithmetic and copies ran while one was open for 10% of the time, Pallas kernels for 0%

commit v1 on v0

v1 whole, which is shorter than its diff:
```python
import jax
import jax.numpy as jnp
from jax import lax
from jax.sharding import PartitionSpec as P

HEADS = 12


def passed_along(x, axis, by):
    count = lax.axis_size(axis)
    pairs = [(i, i + by) for i in range(count) if 0 <= i + by < count]
    return lax.ppermute(x, axis, pairs)


def matmul(left, right):
    return lax.dot_general(
        left, right, (((left.ndim - 1,), (0,)), ((), ())), preferred_element_type=jnp.float32
    )


def against(left, right):
    return lax.dot_general(
        left, right, (((left.ndim - 1,), (1,)), ((), ())), preferred_element_type=jnp.float32
    )


def inner_rows(left, right):
    return lax.dot_general(
        left, right, (((0,), (0,)), ((), ())), preferred_element_type=jnp.float32
    )


def norm_parts(field):
    center = field - jnp.mean(field, axis=-1, keepdims=True)
    inverse = lax.rsqrt(jnp.mean(center * center, axis=-1, keepdims=True) + 1e-06)
    return (center * inverse, inverse)


def norm_back(normed, inverse, upstream):
    return inverse * (
        upstream
        - jnp.mean(upstream, axis=-1, keepdims=True)
        - normed * jnp.mean(upstream * normed, axis=-1, keepdims=True)
    )


def smooth_gate(value):
    return jax.nn.gelu(value, approximate=True)


def dots(pattern, left, right):
    return jnp.einsum(pattern, left, right, preferred_element_type=jnp.float32)


def by_head(rows, count):
    lats, length, width = rows.shape
    return rows.reshape(lats, length, count, width // count)


def attend_forward(queries, key_rows, values, factor):
    scores = dots("bqhd,bkhd->bhqk", queries, key_rows) * factor
    summit = jnp.max(scores, axis=-1, keepdims=True)
    raised = jnp.exp(scores - summit)
    probs = raised / jnp.sum(raised, axis=-1, keepdims=True)
    attended = dots("bhqk,bkhd->bqhd", probs.astype(jnp.bfloat16), values)
    return (attended.astype(jnp.bfloat16), probs)


def attend_backward(queries, key_rows, values, probs, d_attended, factor):
    d_probs = dots("bqhd,bkhd->bhqk", d_attended, values)
    delta = jnp.sum(probs * d_probs, axis=-1, keepdims=True)
    d_scores = (probs * (d_probs - delta)).astype(jnp.bfloat16)
    d_queries = dots("bhqk,bkhd->bqhd", d_scores, key_rows) * factor
    d_keys = dots("bhqk,bqhd->bkhd", d_scores, queries) * factor
    d_values = dots("bhqk,bqhd->bkhd", probs.astype(jnp.bfloat16), d_attended)
    return tuple(part.astype(jnp.bfloat16) for part in (d_queries, d_keys, d_values))


def local(
    section_input,
    timesteps,
    labels,
    time_table,
    label_table,
    w_ada,
    b_ada,
    w_qkv,
    b_qv,
    w_out,
    b_out,
    w_up,
    b_up,
    w_down,
    b_down,
    out_grad,
):
    section = lax.axis_index("pipe")
    shard = lax.axis_index("fsdp")
    shards = lax.axis_size("fsdp")
    groups = lax.axis_size("seq")
    lats, seq_dev, width = section_input.shape
    rows = lats * seq_dev
    full_seq = seq_dev * groups
    heads = HEADS // groups
    head_size = width // HEADS
    band = heads * head_size
    factor = head_size ** (-0.5)
    depth = w_qkv.shape[1]
    hidden_width = w_up.shape[2]

    ids = lax.all_gather(jnp.stack([timesteps, labels]), "fsdp", axis=1, tiled=True)
    bias_sizes = [item.shape[1] for item in (b_ada, b_qv, b_out, b_up, b_down)]
    biases = lax.all_gather(
        jnp.concatenate([b_ada[0], b_qv[0], b_out[0], b_up[0], b_down[0]]), "fsdp", axis=0
    )
    bias_full = []
    start = 0
    for size in bias_sizes:
        bias_full.append(biases[:, start : start + size].reshape(-1).astype(jnp.float32))
        start += size
    ada_bias, joined_bias, out_bias, up_bias, down_bias = bias_full

    by_group = w_qkv[0].reshape(depth, 3, groups, band).transpose(2, 0, 1, 3)
    joined_weight = lax.all_gather(
        by_group.reshape(groups, depth, 3 * band), "fsdp", axis=1, tiled=True
    )
    out_weight = lax.all_gather(w_out[0], "fsdp", axis=0, tiled=True).reshape(groups, band, width)
    up_weight = lax.all_gather(w_up[0], "fsdp", axis=0, tiled=True)
    down_weight = lax.all_gather(w_down[0], "fsdp", axis=0, tiled=True)
    bias_qkv = jnp.stack(
        [joined_bias[:width], jnp.zeros((width,), jnp.float32), joined_bias[width:]]
    )
    bias_qkv = bias_qkv.reshape(3, groups, band).transpose(1, 0, 2).reshape(groups, 1, 3 * band)

    time_hot = (ids[0][:, None] == jnp.arange(time_table.shape[0])[None, :]).astype(jnp.bfloat16)
    label_hot = (ids[1][:, None] == jnp.arange(label_table.shape[0])[None, :]).astype(jnp.bfloat16)
    cond = matmul(time_hot, time_table) + matmul(label_hot, label_table)
    scaled = jax.nn.silu(cond).astype(jnp.bfloat16)
    ada_terms = matmul(scaled, w_ada[0]).reshape(shards, lats, 6 * width)
    modulation = jnp.sum(lax.all_to_all(ada_terms, "fsdp", 0, 0), axis=0) + ada_bias
    shift1, scale1, gate1, shift2, scale2, gate2 = (
        part[:, None] for part in jnp.split(modulation, 6, axis=-1)
    )

    def to_heads(item):
        traded = lax.all_to_all(item, "seq", 0, 0)
        span = traded.shape[-1]
        traded = traded.reshape(groups, lats, seq_dev, span).transpose(1, 0, 2, 3)
        return traded.reshape(lats, full_seq, span)

    def to_tokens(item):
        span = item.shape[-1]
        item = item.reshape(lats, groups, seq_dev, span).transpose(1, 0, 2, 3)
        return lax.all_to_all(item.reshape(groups, rows, span), "seq", 0, 0)

    def flat(item):
        return item.reshape(rows, item.shape[-1])

    def tall(item):
        return item.reshape(lats, seq_dev, item.shape[-1])

    def section_forward(field):
        normed, inverse = norm_parts(field)
        first_in = (normed * (1.0 + scale1) + shift1).astype(jnp.bfloat16)
        joined = (dots("rd,pde->pre", flat(first_in), joined_weight) + bias_qkv).astype(
            jnp.bfloat16
        )
        joined = to_heads(joined)
        parts = tuple(by_head(part, heads) for part in jnp.split(joined, 3, axis=-1))
        attended, probs = attend_forward(*parts, factor)
        back = to_tokens(attended.reshape(lats, full_seq, band))
        branch = tall(dots("pre,pef->rf", back, out_weight) + out_bias)
        middle = field + gate1 * branch
        normed_mid, inverse_mid = norm_parts(middle)
        second_in = (normed_mid * (1.0 + scale2) + shift2).astype(jnp.bfloat16)
        hidden = matmul(flat(second_in), up_weight) + up_bias
        active = smooth_gate(hidden).astype(jnp.bfloat16)
        result = tall(matmul(active, down_weight) + down_bias)
        output = (middle + gate2 * result).astype(jnp.bfloat16)
        kept = (
            (normed, inverse, first_in),
            parts + (probs,),
            back,
            branch,
            (normed_mid, inverse_mid, second_in),
            hidden,
            active,
            result,
        )
        return (output, kept)

    def section_backward(upstream, kept):
        first, attention, back, branch, second, hidden, active, result = kept
        normed, inverse, first_in = first
        normed_mid, inverse_mid, second_in = second
        d_result = (gate2 * upstream).astype(jnp.bfloat16)
        d_active = against(flat(d_result), down_weight)
        _, gate_pull = jax.vjp(smooth_gate, hidden)
        d_hidden = gate_pull(d_active)[0].astype(jnp.bfloat16)
        d_second = tall(against(d_hidden, up_weight))
        d_middle = upstream + norm_back(normed_mid, inverse_mid, d_second * (1.0 + scale2))
        d_branch = (gate1 * d_middle).astype(jnp.bfloat16)
        d_back = dots("rf,pef->pre", flat(d_branch), out_weight).astype(jnp.bfloat16)
        d_parts = attend_backward(*attention, by_head(to_heads(d_back), heads), factor)
        d_joined = to_tokens(
            jnp.concatenate([part.reshape(lats, full_seq, band) for part in d_parts], axis=-1)
        )
        d_first = tall(dots("pre,pde->rd", d_joined, joined_weight))
        d_field = d_middle + norm_back(normed, inverse, d_first * (1.0 + scale1))
        d_field = d_field.astype(jnp.bfloat16)
        sums = (d_first, d_first * normed, d_middle * branch, d_second, d_second * normed_mid)
        d_mods = jnp.concatenate(
            [jnp.sum(item, axis=1) for item in sums + (upstream * result,)], axis=-1
        )
        return (d_field, d_mods, (d_joined, d_branch, d_hidden, d_result))

    handed, _ = section_forward(section_input.astype(jnp.float32))
    handed = passed_along(handed, "pipe", 1)
    entering = jnp.where(section == 0, section_input, handed)
    section_out, kept = section_forward(entering.astype(jnp.float32))
    handed, _, _ = section_backward(out_grad.astype(jnp.float32), kept)
    handed = passed_along(handed, "pipe", -1)
    upstream = jnp.where(section == 1, out_grad, handed).astype(jnp.float32)
    section_in_grad, d_mods, d_parts = section_backward(upstream, kept)
    d_joined, d_branch, d_hidden, d_result = d_parts
    d_branch, d_result = flat(d_branch), flat(d_result)

    def over_shards(part, dim):
        return lax.psum_scatter(
            part.astype(jnp.bfloat16), "fsdp", scatter_dimension=dim, tiled=True
        )

    in_order = d_joined.reshape(groups, rows, 3, band).transpose(1, 2, 0, 3)
    in_order = in_order.reshape(rows, 3 * width)
    grad_down = over_shards(inner_rows(kept[6], d_result), 0)
    grad_up = over_shards(inner_rows(flat(kept[4][2]), d_hidden), 0)
    grad_joined = over_shards(inner_rows(flat(kept[0][2]), in_order), 0)
    grad_out = over_shards(dots("pre,rf->pef", kept[2], d_branch).reshape(width, width), 0)
    def over_tokens(part):
        cut_up = part.reshape((groups, part.shape[0] // groups) + part.shape[1:])
        terms = lax.all_to_all(cut_up, "seq", 0, 0).astype(jnp.float32)
        own = jnp.sum(terms, axis=0).astype(jnp.bfloat16)
        whole = lax.all_to_all(jnp.broadcast_to(own[None], cut_up.shape), "seq", 0, 0)
        return whole.reshape(part.shape).astype(jnp.float32)

    grad_down = over_tokens(grad_down)
    grad_up = over_tokens(grad_up)
    grad_joined = over_tokens(grad_joined)
    grad_out = over_tokens(grad_out)

    placed = lax.dynamic_update_slice(
        jnp.zeros((shards * lats, 6 * width), jnp.float32), d_mods, (shard * lats, 0)
    )
    joined_sums = jnp.sum(d_joined, axis=1, dtype=jnp.float32).reshape(groups, 3, band)
    qv_sums = jnp.stack([joined_sums[:, 0], joined_sums[:, 2]])
    column_sums = [
        qv_sums.reshape(-1),
        jnp.sum(d_branch, axis=0, dtype=jnp.float32),
        jnp.sum(d_hidden, axis=0, dtype=jnp.float32),
        jnp.sum(d_result, axis=0, dtype=jnp.float32),
    ]
    small = lax.psum(jnp.concatenate([placed.reshape(-1)] + column_sums), ("fsdp", "seq"))
    cut = placed.size
    d_modulation = small[:cut].reshape(placed.shape).astype(jnp.bfloat16)

    def own_part(whole):
        size = whole.shape[0] // shards
        return lax.dynamic_slice_in_dim(whole, shard * size, size, 0)[None]

    bias_grads = []
    for part in column_sums:
        bias_grads.append(own_part(small[cut : cut + part.size]))
        cut += part.size
    grad_ada = inner_rows(scaled, d_modulation)
    grad_ada_bias = own_part(jnp.sum(d_modulation, axis=0, dtype=jnp.float32))
    d_scaled = against(d_modulation, w_ada[0])
    other = lax.ppermute(d_scaled, "pipe", [(0, 1), (1, 0)])
    _, silu_pull = jax.vjp(jax.nn.silu, cond)
    d_cond = silu_pull(d_scaled + other)[0]

    def table_grad(hot):
        return lax.dot_general(
            hot.astype(jnp.float32),
            d_cond,
            (((0,), (0,)), ((), ())),
            precision=lax.Precision.HIGHEST,
        )

    return (
        section_out[None],
        section_in_grad[None],
        table_grad(time_hot),
        table_grad(label_hot),
        grad_ada[None],
        grad_ada_bias,
        grad_joined[None],
        bias_grads[0],
        grad_out[None],
        bias_grads[1],
        grad_up[None],
        bias_grads[2],
        grad_down[None],
        bias_grads[3],
    )


def solution(mesh):
    in_specs = (
        P("fsdp", "seq", None),
        P("fsdp"),
        P("fsdp"),
        P(None, "fsdp"),
        P(None, "fsdp"),
        P("pipe", "fsdp", None),
        P("pipe", "fsdp"),
        P("pipe", "fsdp", None),
        P("pipe", "fsdp"),
        P("pipe", "fsdp", None),
        P("pipe", "fsdp"),
        P("pipe", "fsdp", None),
        P("pipe", "fsdp"),
        P("pipe", "fsdp", None),
        P("pipe", "fsdp"),
        P("fsdp", "seq", None),
    )
    out_specs = (
        P("pipe", "fsdp", "seq", None),
        P("pipe", "fsdp", "seq", None),
        P(None, "fsdp"),
        P(None, "fsdp"),
        P("pipe", "fsdp", None),
        P("pipe", "fsdp"),
        P("pipe", "fsdp", None),
        P("pipe", "fsdp"),
        P("pipe", "fsdp", None),
        P("pipe", "fsdp"),
        P("pipe", "fsdp", None),
        P("pipe", "fsdp"),
        P("pipe", "fsdp", None),
        P("pipe", "fsdp"),
    )
    return jax.shard_map(local, mesh=mesh, in_specs=in_specs, out_specs=out_specs, check_vma=False)
```

time: 1460 us -> 823 us (0.56)
  waiting for transfers between devices: 911 us -> 447 us
  local copies, waits for them, and re-layouts: 197 us -> 67.2 us
  matrix products: 127 us -> 86.1 us
  blocking collectives: 75.9 us -> 112 us
  other arithmetic: 60.5 us -> 38 us
    reduce_scatter x7 -> x4, waiting for transfers between devices: 278 us -> 82.1 us  [over_shards(): lax.psum_scatter(part.astype(jnp.bfloat16), 'fsdp', scatter_dimension=dim...]
    unnamed x25 -> x9, waiting for transfers between devices: 142 us -> 2 us
    all_gather x7 -> x4, waiting for transfers between devices: 248 us -> 132 us  [the longest x1 58.8 us: local(): up_weight = lax.all_gather(w_up[0], 'fsdp', axis=0, tiled=True)]
    all_to_all x0 -> x6, blocking collectives: none -> 93.6 us  [the longest x3 51.4 us: to_heads(): traded = lax.all_to_all(item, 'seq', 0, 0)]
    psum x1, waiting for transfers between devices: 196 us -> 117 us  [local(): lax.psum(jnp.concatenate([placed.reshape(-1)] + column_sums), ('fsdp', 's...]
    all_to_all x12 -> x11, waiting for transfers between devices: 44.7 us -> 113 us  [the longest x3 48.7 us: over_tokens(): terms = lax.all_to_all(cut_up, 'seq', 0, 0).astype(jnp.float32)]
    unnamed x371 -> x185, local copies, waits for them, and re-layouts: 73.7 us -> 10.4 us
    psum x3 -> x0, blocking collectives: 42 us -> none  [the longest x1 21.9 us: local(): lax.psum(for_sending(shards), 'seq')]
  transfers between devices with their start and end apart: 36 -> 23, of which waited for: 29 -> 16; matrix products, arithmetic and copies ran while one was open for 10% -> 10% of each run, Pallas kernels for 0% -> 0%
where the time goes in v1:
time: 823 us; the launch traced here: 813 us
  waiting for transfers between devices  447 us (54%)
  blocking collectives  112 us (14%)
  matrix products  86.1 us (10%)
  local copies, waits for them, and re-layouts  67.2 us (8%)
  starting transfers between devices  47.5 us (6%)
  other arithmetic  38 us (5%)
  between operations  15.3 us (2%)
    psum x1, waiting for transfers between devices, local(): lax.psum(jnp.concatenate([placed.reshape(-1)] + column_sums), ('fsdp', 's...  117 us
    reduce_scatter x4, waiting for transfers between devices, over_shards(): lax.psum_scatter(part.astype(jnp.bfloat16), 'fsdp', scatter_dimension=dim...  82.1 us
    all_gather x1, waiting for transfers between devices, local(): up_weight = lax.all_gather(w_up[0], 'fsdp', axis=0, tiled=True)  58.8 us
    all_to_all x3, blocking collectives, to_heads(): traded = lax.all_to_all(item, 'seq', 0, 0)  51.4 us
    all_to_all x3, waiting for transfers between devices, over_tokens(): terms = lax.all_to_all(cut_up, 'seq', 0, 0).astype(jnp.float32)  48.7 us
    all_gather x1, waiting for transfers between devices, local(): down_weight = lax.all_gather(w_down[0], 'fsdp', axis=0, tiled=True)  45.8 us
    all_to_all x4, waiting for transfers between devices, over_tokens(): lax.all_to_all(jnp.broadcast_to(own[None], cut_up.shape), 'seq', 0, 0)  38.5 us
    dot_general x19, matrix products, dots(): return jnp.einsum(pattern, left, right, preferred_element_type=jnp.float32)  35.5 us
  transfers between devices with their start and end apart: 23, of which 16 were waited for; matrix products, arithmetic and copies ran while one was open for 10% of the time, Pallas kernels for 0%

profile of v1, /device:TPU:0, one launch (start us, length us, event | category | flops | bytes accessed | tf_op | source)
XLA Modules:
  0.0 812.8 jit_solution(12750251277697999623)
XLA Ops:
  16.6 9.5 %all-gather.4 = s32[4,2,2]{2,1,0:T(2,128)S(1)} all-gather(s32[1,2,2]{2,1,0:T(2,128)S(1)} %bitcast.395), channel_id=1, replica_groups=mesh['pipe'=2,'seq'=4,'fsdp'=4] {'fsdp'}, dimensions={0}, use_global_device_ids=true | all-gather | bytes 80 | tf_op jit(solution)/shard_map/all_gather | solution.py:111
  32.9 8.8 %all-gather.5 = bf16[4,1,2688]{2,1,0:T(2,128)(2,1)S(1)} all-gather(bf16[1,1,2688]{2,1,0:T(2,128)(2,1)S(1)} %reshape.480), channel_id=2, replica_groups=mesh['pipe'=2,'seq'=4,'fsdp'=4] {'fsdp'}, dimensions={0}, use_global_device_ids=true | all-gather | bytes 26880 | tf_op jit(solution)/shard_map/all_gather | solution.py:113
  42.8 27.3 %all-gather.11.cloned.1.call-done = bf16[4,768,576]{2,1,0:T(8,128)(2,1)} async-done(((bf16[4,192,576]{2,1,0:T(8,128)(2,1)}), bf16[4,768,576]{2,1,0:T(8,128)(2,1)}) %all-gather.11.cloned.1.call-update) | async-done | bytes 3538960 | tf_op jit(solution)/shard_map/all_gather | solution.py:124
  73.8 20.3 %all_to_all.85 = bf16[4,128,576]{1,2,0:T(8,128)(2,1)S(1)} all-to-all(bf16[4,128,576]{1,2,0:T(8,128)(2,1)S(1)} %fusion.55), channel_id=1, replica_groups=mesh['pipe'=2,'seq'=4,'fsdp'=4] {'seq'}, dimensions={0} | all-to-all | bytes 1179648 | tf_op jit(solution)/shard_map/all_to_all | solution.py:146
  103.5 6.9 all-to-all-done.2
  112.9 45.8 %all-gather.17.cloned.1.call-done = bf16[1,3072,768]{2,1,0:T(8,128)(2,1)} async-done(((bf16[1,768,768]{2,1,0:T(8,128)(2,1)}), bf16[1,3072,768]{2,1,0:T(8,128)(2,1)}) %all-gather.17.cloned.1.call-update) | async-done | bytes 4718608 | tf_op jit(solution)/shard_map/all_gather | solution.py:129
  158.7 58.8 %all-gather.15.cloned.1.call-done = bf16[1,768,3072]{2,1,0:T(8,128)(2,1)} async-done(((bf16[1,192,3072]{2,1,0:T(8,128)(2,1)}), bf16[1,768,3072]{2,1,0:T(8,128)(2,1)}) %all-gather.15.cloned.1.call-update) | async-done | bytes 4718608 | tf_op jit(solution)/shard_map/all_gather | solution.py:128
  217.5 5.6 fusion.56
  231.0 20.8 %all_to_all.86 = bf16[4,128,576]{1,2,0:T(8,128)(2,1)S(1)} all-to-all(bf16[4,128,576]{1,2,0:T(8,128)(2,1)S(1)} %fusion.54), channel_id=1, replica_groups=mesh['pipe'=2,'seq'=4,'fsdp'=4] {'seq'}, dimensions={0} | all-to-all | bytes 1179648 | tf_op jit(solution)/shard_map/all_to_all | solution.py:146
  263.5 10.0 %all_to_all.87 = bf16[4,128,192]{1,2,0:T(8,128)(2,1)S(1)} all-to-all(bf16[4,128,192]{1,2,0:T(8,128)(2,1)S(1)} %copy.188), channel_id=1, replica_groups=mesh['pipe'=2,'seq'=4,'fsdp'=4] {'seq'}, dimensions={0} | all-to-all | bytes 393216 | tf_op jit(solution)/shard_map/all_to_all | solution.py:154
  281.0 8.7 %fusion.113 = (f32[128]{0:T(128)}, f32[128,768]{1,0:T(8,128)}) fusion(f32[2,768]{1,0:T(2,128)S(1)} %get-tuple-element.44, bf16[1,768,3072]{2,1,0:T(8,128)(2,1)} %all-gather.15.cloned.1.call-done, f32[128,3072]{1,0:T(8,128)} %fusion.21, bf16[128,768]{1,0:T(8,128)(2,1)} %bitcast.377, bf16[1,3072,768]{2,1,0:T(8,128)(2,1)} %all-gather.17.cloned.1.call-done), kind=kOutput, calls=%fused_computation.151 | convolution fusion | flops 1216020352 | bytes 11606528 | tf_op jit(solution)/shard_map/dot_general | solution.py:22
  295.9 10.2 %all_to_all.88 = bf16[4,128,192]{1,2,0:T(8,128)(2,1)} all-to-all(bf16[4,128,192]{1,2,0:T(8,128)(2,1)S(1)} %fusion.72), channel_id=1, replica_groups=mesh['pipe'=2,'seq'=4,'fsdp'=4] {'seq'}, dimensions={0} | all-to-all | bytes 393216 | tf_op jit(solution)/shard_map/all_to_all | solution.py:146
  335.4 14.0 %all-to-all-done.6 = bf16[4,128,576]{1,2,0:T(8,128)(2,1)} async-done(((bf16[4,128,576]{1,2,0:T(8,128)(2,1)}), bf16[4,128,576]{1,2,0:T(8,128)(2,1)}, u32[]{:S(2)}, u32[]{:S(2)}) %all-to-all-start.6) | async-done | bytes 589856 | tf_op jit(solution)/shard_map/all_to_all | solution.py:154
  385.1 5.2 all-to-all-done.7
  411.2 19.8 %all_to_all.89 = bf16[4,128,576]{1,2,0:T(8,128)(2,1)S(1)} all-to-all(bf16[4,128,576]{1,2,0:T(8,128)(2,1)S(1)} %copy.202), channel_id=1, replica_groups=mesh['pipe'=2,'seq'=4,'fsdp'=4] {'seq'}, dimensions={0} | all-to-all | bytes 1179648 | tf_op jit(solution)/shard_map/all_to_all | solution.py:154
  445.7 12.5 %all_to_all.90 = bf16[4,48,768]{2,1,0:T(8,128)(2,1)S(1)} all-to-all(bf16[4,48,768]{2,1,0:T(8,128)(2,1)} %bitcast.381), channel_id=1, replica_groups=mesh['pipe'=2,'seq'=4,'fsdp'=4] {'seq'}, dimensions={0} | all-to-all | bytes 589824 | tf_op jit(solution)/shard_map/all_to_all | solution.py:241
  458.2 22.1 %reduce-scatter.5.cloned.1.call-done = bf16[192,2304]{1,0:T(8,128)(2,1)} async-done(((bf16[768,2304]{1,0:T(8,128)(2,1)}), bf16[192,2304]{1,0:T(8,128)(2,1)}) %reduce-scatter.5.cloned.1.call-update) | async-done | bytes 884752 | tf_op jit(solution)/shard_map/reduce_scatter | solution.py:229
  484.9 22.2 %all-to-all-done.9 = bf16[4,48,2304]{2,1,0:T(8,128)(2,1)S(1)} async-done(((bf16[4,48,2304]{2,1,0:T(8,128)(2,1)}), bf16[4,48,2304]{2,1,0:T(8,128)(2,1)S(1)}, u32[]{:S(2)}, u32[]{:S(2)}) %all-to-all-start.9) | async-done | bytes 884768 | tf_op jit(solution)/shard_map/all_to_all | solution.py:241
  511.5 8.9 %all-to-all-done.12 = bf16[4,48,768]{2,1,0:T(8,128)(2,1)S(1)} async-done(((bf16[4,48,768]{2,1,0:T(8,128)(2,1)}), bf16[4,48,768]{2,1,0:T(8,128)(2,1)S(1)}, u32[]{:S(2)}, u32[]{:S(2)}) %all-to-all-start.12) | async-done | bytes 294944 | tf_op jit(solution)/shard_map/all_to_all | solution.py:243
  525.0 15.4 %reduce-scatter.9.cloned.1.call-done = bf16[192,3072]{1,0:T(8,128)(2,1)} async-done(((bf16[768,3072]{1,0:T(8,128)(2,1)}), bf16[192,3072]{1,0:T(8,128)(2,1)}) %reduce-scatter.9.cloned.1.call-update) | async-done | bytes 1179664 | tf_op jit(solution)/shard_map/reduce_scatter | solution.py:229
  556.0 44.6 %reduce-scatter.11.cloned.1.call-done = bf16[768,768]{1,0:T(8,128)(2,1)} async-done(((bf16[3072,768]{1,0:T(8,128)(2,1)}), bf16[768,768]{1,0:T(8,128)(2,1)}) %reduce-scatter.11.cloned.1.call-update) | async-done | bytes 1179664 | tf_op jit(solution)/shard_map/reduce_scatter | solution.py:229
  607.2 26.5 %all-to-all-done.15 = bf16[4,192,768]{2,1,0:T(8,128)(2,1)} async-done(((bf16[4,192,768]{2,1,0:T(8,128)(2,1)}), bf16[4,192,768]{2,1,0:T(8,128)(2,1)}, u32[]{:S(2)}, u32[]{:S(2)}) %all-to-all-start.15) | async-done | bytes 1179680 | tf_op jit(solution)/shard_map/all_to_all | solution.py:241
  639.6 116.7 %all-reduce.2.cloned.1.call-done = f32[43008]{0:T(1024)} async-done(((f32[43008]{0:T(1024)}), f32[43008]{0:T(1024)}) %all-reduce.2.cloned.1.call-update) | async-done | bytes 172048 | tf_op jit(solution)/shard_map/psum | solution.py:262
  778.7 24.5 %all-to-all-done.16 = bf16[4,192,768]{2,1,0:T(8,128)(2,1)} async-done(((bf16[4,192,768]{2,1,0:T(8,128)(2,1)}), bf16[4,192,768]{2,1,0:T(8,128)(2,1)}, u32[]{:S(2)}, u32[]{:S(2)}) %all-to-all-start.16) | async-done | bytes 1179680 | tf_op jit(solution)/shard_map/all_to_all | solution.py:243
  (411 shorter events, 232.3 us)
Async XLA Ops:
  7.2 62.9 %all-gather.11.cloned.1.call-start = ((), (), s32[]{:S(2)}) async-start(), calls=%async_computation.21 | async-start | bytes 4915200 | tf_op jit(solution)/shard_map/all_gather | solution.py:124
  14.9 88.6 %all-gather.13.cloned.1.call-start = ((), (), s32[]{:S(2)}) async-start(), calls=%async_computation.27 | async-start | bytes 1474560 | tf_op jit(solution)/shard_map/all_gather | solution.py:127
  15.7 143.0 %all-gather.17.cloned.1.call-start = ((), (), s32[]{:S(2)}) async-start(), calls=%async_computation.29 | async-start | bytes 5898240 | tf_op jit(solution)/shard_map/all_gather | solution.py:129
  28.7 13.8 %all-to-all-start = ((f32[4,2,4608]{2,1,0:T(2,128)}), f32[4,2,4608]{2,1,0:T(2,128)S(1)}, u32[]{:S(2)}, u32[]{:S(2)}) async-start(f32[4,2,4608]{2,1,0:T(2,128)} %fusion.24), calls=%async_computation | async-start | bytes 294912 | tf_op jit(solution)/shard_map/all_to_all | solution.py:140
  32.0 185.4 %all-gather.15.cloned.1.call-start = ((), (), s32[]{:S(2)}) async-start(), calls=%async_computation.28 | async-start | bytes 5898240 | tf_op jit(solution)/shard_map/all_gather | solution.py:128
  42.6 180.4 %copy-start.35 = (f32[2,768]{1,0:T(2,128)}, f32[2,768]{1,0:T(2,128)S(1)}, u32[]{:S(2)}) copy-start(f32[2,768]{1,0:T(2,128)S(1)} %get-tuple-element.47) | copy-start | bytes 18436
  99.8 10.6 %all-to-all-start.2 = ((bf16[4,128,192]{1,2,0:T(8,128)(2,1)}), bf16[4,128,192]{1,2,0:T(8,128)(2,1)S(1)}, u32[]{:S(2)}, u32[]{:S(2)}) async-start(bf16[4,128,192]{1,2,0:T(8,128)(2,1)} %copy.180), calls=%async_computation.2 | async-start | bytes 393216 | tf_op jit(solution)/shard_map/all_to_all | solution.py:154
  223.9 2.8 collective-permute-start
  331.2 18.2 %all-to-all-start.6 = ((bf16[4,128,576]{1,2,0:T(8,128)(2,1)}), bf16[4,128,576]{1,2,0:T(8,128)(2,1)}, u32[]{:S(2)}, u32[]{:S(2)}) async-start(bf16[4,128,576]{1,2,0:T(8,128)(2,1)} %copy.195), calls=%async_computation.6 | async-start | bytes 1179648 | tf_op jit(solution)/shard_map/all_to_all | solution.py:154
  358.3 5.7 collective-permute-start.1
  378.4 11.9 %all-to-all-start.7 = ((bf16[4,128,192]{1,2,0:T(8,128)(2,1)}), bf16[4,128,192]{1,2,0:T(8,128)(2,1)}, u32[]{:S(2)}, u32[]{:S(2)}) async-start(bf16[4,128,192]{1,2,0:T(8,128)(2,1)} %fusion.73), calls=%async_computation.7 | async-start | bytes 393216 | tf_op jit(solution)/shard_map/all_to_all | solution.py:146
  382.4 63.3 %reduce-scatter.7.cloned.1.call-start = ((), (), s32[]{:S(2)}) async-start(), calls=%async_computation.24 | async-start | bytes 1474560 | tf_op jit(solution)/shard_map/reduce_scatter | solution.py:229
  384.9 95.4 %reduce-scatter.5.cloned.1.call-start = ((), (), s32[]{:S(2)}) async-start(), calls=%async_computation.23 | async-start | bytes 4423680 | tf_op jit(solution)/shard_map/reduce_scatter | solution.py:229
  434.8 105.6 %reduce-scatter.9.cloned.1.call-start = ((), (), s32[]{:S(2)}) async-start(), calls=%async_computation.25 | async-start | bytes 5898240 | tf_op jit(solution)/shard_map/reduce_scatter | solution.py:229
  439.6 161.0 %reduce-scatter.11.cloned.1.call-start = ((), (), s32[]{:S(2)}) async-start(), calls=%async_computation.26 | async-start | bytes 5898240 | tf_op jit(solution)/shard_map/reduce_scatter | solution.py:229
  480.3 26.8 %all-to-all-start.9 = ((bf16[4,48,2304]{2,1,0:T(8,128)(2,1)}), bf16[4,48,2304]{2,1,0:T(8,128)(2,1)S(1)}, u32[]{:S(2)}, u32[]{:S(2)}) async-start(bf16[4,48,2304]{2,1,0:T(8,128)(2,1)} %bitcast.374), calls=%async_computation.10 | async-start | bytes 1769472 | tf_op jit(solution)/shard_map/all_to_all | solution.py:241
  507.9 12.5 %all-to-all-start.12 = ((bf16[4,48,768]{2,1,0:T(8,128)(2,1)}), bf16[4,48,768]{2,1,0:T(8,128)(2,1)S(1)}, u32[]{:S(2)}, u32[]{:S(2)}) async-start(bf16[4,48,768]{2,1,0:T(8,128)(2,1)} %broadcast_in_dim.33), calls=%async_computation.14 | async-start | bytes 589824 | tf_op jit(solution)/shard_map/all_to_all | solution.py:243
  521.4 24.1 %all-to-all-start.10 = ((bf16[4,48,2304]{2,1,0:T(8,128)(2,1)}), bf16[4,48,2304]{2,1,0:T(8,128)(2,1)S(1)}, u32[]{:S(2)}, u32[]{:S(2)}) async-start(bf16[4,48,2304]{2,1,0:T(8,128)(2,1)} %broadcast_in_dim.31), calls=%async_computation.11 | async-start | bytes 1769472 | tf_op jit(solution)/shard_map/all_to_all | solution.py:243
  545.5 55.1 %all-to-all-start.13 = ((bf16[4,48,3072]{2,1,0:T(8,128)(2,1)}), bf16[4,48,3072]{2,1,0:T(8,128)(2,1)}, u32[]{:S(2)}, u32[]{:S(2)}) async-start(bf16[4,48,3072]{2,1,0:T(8,128)(2,1)} %bitcast.369), calls=%async_computation.16 | async-start | bytes 2359296 | tf_op jit(solution)/shard_map/all_to_all | solution.py:241
  600.5 33.2 %all-to-all-start.15 = ((bf16[4,192,768]{2,1,0:T(8,128)(2,1)}), bf16[4,192,768]{2,1,0:T(8,128)(2,1)}, u32[]{:S(2)}, u32[]{:S(2)}) async-start(bf16[4,192,768]{2,1,0:T(8,128)(2,1)} %bitcast.368), calls=%async_computation.19 | async-start | bytes 2359296 | tf_op jit(solution)/shard_map/all_to_all | solution.py:241
  634.9 133.4 %all-to-all-start.14 = ((bf16[4,48,3072]{2,1,0:T(8,128)(2,1)}), bf16[4,48,3072]{2,1,0:T(8,128)(2,1)S(1)}, u32[]{:S(2)}, u32[]{:S(2)}) async-start(bf16[4,48,3072]{2,1,0:T(8,128)(2,1)} %broadcast_in_dim.35), calls=%async_computation.17 | async-start | bytes 2359296 | tf_op jit(solution)/shard_map/all_to_all | solution.py:243
  638.6 117.8 %all-reduce.2.cloned.1.call-start = ((), (), s32[]{:S(2)}) async-start(), calls=%async_computation.22 | async-start | bytes 344064 | tf_op jit(solution)/shard_map/psum | solution.py:262
  758.0 5.9 collective-permute-start.2
  769.4 33.8 %all-to-all-start.16 = ((bf16[4,192,768]{2,1,0:T(8,128)(2,1)}), bf16[4,192,768]{2,1,0:T(8,128)(2,1)}, u32[]{:S(2)}, u32[]{:S(2)}) async-start(bf16[4,192,768]{2,1,0:T(8,128)(2,1)} %broadcast_in_dim.37), calls=%async_computation.20 | async-start | bytes 2359296 | tf_op jit(solution)/shard_map/all_to_all | solution.py:243
  (86 other events, 1137.4 us)
Sparse Core Ops, SparseCore 0:
  15.1 55.0 all-gather.10
  72.0 27.7 all-gather.12
  101.6 57.0 all-gather.16
  160.4 57.0 all-gather.14
  385.9 29.4 reduce-scatter.6
  434.9 45.3 reduce-scatter.4
  483.3 57.0 reduce-scatter.8
  543.4 57.0 reduce-scatter.10
  645.3 111.0 all-reduce.1

commit v2 on v1

--- a/solution.py
+++ b/solution.py
@@ -189,22 +189,35 @@
         )
         return (output, kept)
 
-    def section_backward(upstream, kept):
+    def over_shards(part):
+        return lax.psum_scatter(part, "fsdp", scatter_dimension=0, tiled=True)
+
+    def held_first(left, right, wanted):
+        if not wanted:
+            return (right, None)
+        term = inner_rows(left, right).astype(jnp.bfloat16)
+        return lax.optimization_barrier((right, term))
+
+    def section_backward(upstream, kept, wanted):
         first, attention, back, branch, second, hidden, active, result = kept
         normed, inverse, first_in = first
         normed_mid, inverse_mid, second_in = second
         d_result = (gate2 * upstream).astype(jnp.bfloat16)
-        d_active = against(flat(d_result), down_weight)
+        d_result, down_term = held_first(active, flat(d_result), wanted)
+        d_active = against(d_result, down_weight)
         _, gate_pull = jax.vjp(smooth_gate, hidden)
         d_hidden = gate_pull(d_active)[0].astype(jnp.bfloat16)
+        d_hidden, up_term = held_first(flat(second_in), d_hidden, wanted)
         d_second = tall(against(d_hidden, up_weight))
         d_middle = upstream + norm_back(normed_mid, inverse_mid, d_second * (1.0 + scale2))
-        d_branch = (gate1 * d_middle).astype(jnp.bfloat16)
-        d_back = dots("rf,pef->pre", flat(d_branch), out_weight).astype(jnp.bfloat16)
+        d_branch = flat((gate1 * d_middle).astype(jnp.bfloat16))
+        d_back = dots("rf,pef->pre", d_branch, out_weight).astype(jnp.bfloat16)
         d_parts = attend_backward(*attention, by_head(to_heads(d_back), heads), factor)
         d_joined = to_tokens(
             jnp.concatenate([part.reshape(lats, full_seq, band) for part in d_parts], axis=-1)
         )
+        if wanted:
+            d_joined, down_term = lax.optimization_barrier((d_joined, over_shards(down_term)))
         d_first = tall(dots("pre,pde->rd", d_joined, joined_weight))
         d_field = d_middle + norm_back(normed, inverse, d_first * (1.0 + scale1))
         d_field = d_field.astype(jnp.bfloat16)
@@ -212,30 +225,25 @@
         d_mods = jnp.concatenate(
             [jnp.sum(item, axis=1) for item in sums + (upstream * result,)], axis=-1
         )
-        return (d_field, d_mods, (d_joined, d_branch, d_hidden, d_result))
+        return (d_field, d_mods, (d_joined, d_branch, d_hidden, d_result), (down_term, up_term))
 
     handed, _ = section_forward(section_input.astype(jnp.float32))
     handed = passed_along(handed, "pipe", 1)
     entering = jnp.where(section == 0, section_input, handed)
     section_out, kept = section_forward(entering.astype(jnp.float32))
-    handed, _, _ = section_backward(out_grad.astype(jnp.float32), kept)
+    handed = section_backward(out_grad.astype(jnp.float32), kept, False)[0]
     handed = passed_along(handed, "pipe", -1)
     upstream = jnp.where(section == 1, out_grad, handed).astype(jnp.float32)
-    section_in_grad, d_mods, d_parts = section_backward(upstream, kept)
+    section_in_grad, d_mods, d_parts, terms = section_backward(upstream, kept, True)
     d_joined, d_branch, d_hidden, d_result = d_parts
-    d_branch, d_result = flat(d_branch), flat(d_result)
-
-    def over_shards(part, dim):
-        return lax.psum_scatter(
-            part.astype(jnp.bfloat16), "fsdp", scatter_dimension=dim, tiled=True
-        )
 
     in_order = d_joined.reshape(groups, rows, 3, band).transpose(1, 2, 0, 3)
     in_order = in_order.reshape(rows, 3 * width)
-    grad_down = over_shards(inner_rows(kept[6], d_result), 0)
-    grad_up = over_shards(inner_rows(flat(kept[4][2]), d_hidden), 0)
-    grad_joined = over_shards(inner_rows(flat(kept[0][2]), in_order), 0)
-    grad_out = over_shards(dots("pre,rf->pef", kept[2], d_branch).reshape(width, width), 0)
+    grad_down = terms[0]
+    grad_up = over_shards(terms[1])
+    grad_joined = over_shards(inner_rows(flat(kept[0][2]), in_order).astype(jnp.bfloat16))
+    out_term = dots("pre,rf->pef", kept[2], d_branch).reshape(width, width)
+    grad_out = over_shards(out_term.astype(jnp.bfloat16))
     def over_tokens(part):
         cut_up = part.reshape((groups, part.shape[0] // groups) + part.shape[1:])
         terms = lax.all_to_all(cut_up, "seq", 0, 0).astype(jnp.float32)
@@ -248,9 +256,6 @@
     grad_joined = over_tokens(grad_joined)
     grad_out = over_tokens(grad_out)
 
-    placed = lax.dynamic_update_slice(
-        jnp.zeros((shards * lats, 6 * width), jnp.float32), d_mods, (shard * lats, 0)
-    )
     joined_sums = jnp.sum(d_joined, axis=1, dtype=jnp.float32).reshape(groups, 3, band)
     qv_sums = jnp.stack([joined_sums[:, 0], joined_sums[:, 2]])
     column_sums = [
@@ -259,20 +264,26 @@
         jnp.sum(d_hidden, axis=0, dtype=jnp.float32),
         jnp.sum(d_result, axis=0, dtype=jnp.float32),
     ]
-    small = lax.psum(jnp.concatenate([placed.reshape(-1)] + column_sums), ("fsdp", "seq"))
-    cut = placed.size
-    d_modulation = small[:cut].reshape(placed.shape).astype(jnp.bfloat16)
-
-    def own_part(whole):
-        size = whole.shape[0] // shards
-        return lax.dynamic_slice_in_dim(whole, shard * size, size, 0)[None]
-
+    small = jnp.concatenate([d_mods.reshape(-1)] + column_sums)
+    small = lax.all_to_all(jnp.broadcast_to(small, (groups, small.size)), "seq", 0, 0)
+    small = jnp.sum(small, axis=0)
+    mods_sum = jnp.broadcast_to(small[: d_mods.size], (shards, d_mods.size))
+    to_shards = [mods_sum]
+    cut = d_mods.size
+    for part in column_sums:
+        to_shards.append(small[cut : cut + part.size].reshape(shards, part.size // shards))
+        cut += part.size
+    small = lax.all_to_all(jnp.concatenate(to_shards, axis=1), "fsdp", 0, 0)
+    d_modulation = small[:, : d_mods.size].reshape(shards * lats, 6 * width).astype(jnp.bfloat16)
     bias_grads = []
-    for part in column_sums:
-        bias_grads.append(own_part(small[cut : cut + part.size]))
-        cut += part.size
+    cut = d_mods.size
+    for part in to_shards[1:]:
+        bias_grads.append(jnp.sum(small[:, cut : cut + part.shape[1]], axis=0)[None])
+        cut += part.shape[1]
+    ada_sums = jnp.sum(d_modulation, axis=0, dtype=jnp.float32)
+    ada_size = 6 * width // shards
+    grad_ada_bias = lax.dynamic_slice_in_dim(ada_sums, shard * ada_size, ada_size, 0)[None]
     grad_ada = inner_rows(scaled, d_modulation)
-    grad_ada_bias = own_part(jnp.sum(d_modulation, axis=0, dtype=jnp.float32))
     d_scaled = against(d_modulation, w_ada[0])
     other = lax.ppermute(d_scaled, "pipe", [(0, 1), (1, 0)])
     _, silu_pull = jax.vjp(jax.nn.silu, cond)

time: 823 us -> 746 us (0.906)
  waiting for transfers between devices: 447 us -> 317 us
  blocking collectives: 112 us -> 155 us
  starting transfers between devices: 47.5 us -> 58.9 us
    psum x1 -> x0, waiting for transfers between devices: 117 us -> none  [local(): lax.psum(jnp.concatenate([placed.reshape(-1)] + column_sums), ('fsdp', 's...]
    reduce_scatter x4, waiting for transfers between devices: 82.1 us -> 49.6 us  [over_shards(): return lax.psum_scatter(part, 'fsdp', scatter_dimension=0, tiled=True)]
    all_to_all x0 -> x1, blocking collectives: none -> 30.5 us  [over_tokens(): lax.all_to_all(jnp.broadcast_to(own[None], cut_up.shape), 'seq', 0, 0)]
    all_to_all x1, blocking collectives: 12.5 us -> 33.2 us  [over_tokens(): terms = lax.all_to_all(cut_up, 'seq', 0, 0).astype(jnp.float32)]
    all_to_all x2 -> x1, blocking collectives: 29.8 us -> 10 us  [to_tokens(): return lax.all_to_all(item.reshape(groups, rows, span), 'seq', 0, 0)]
    all_to_all x2 -> x3, waiting for transfers between devices: 20.9 us -> 37.1 us  [to_tokens(): return lax.all_to_all(item.reshape(groups, rows, span), 'seq', 0, 0)]
    all_gather x1, waiting for transfers between devices: 45.8 us -> 58.8 us  [local(): down_weight = lax.all_gather(w_down[0], 'fsdp', axis=0, tiled=True)]
    all_gather x1, waiting for transfers between devices: 58.8 us -> 45.8 us  [local(): up_weight = lax.all_gather(w_up[0], 'fsdp', axis=0, tiled=True)]
  transfers between devices with their start and end apart: 23 -> 23, of which waited for: 16 -> 15; matrix products, arithmetic and copies ran while one was open for 10% -> 9% of each run, Pallas kernels for 0% -> 0%
where the time goes in v2:
time: 746 us; the launch traced here: 740 us
  waiting for transfers between devices  317 us (42%)
  blocking collectives  155 us (21%)
  matrix products  87.9 us (12%)
  local copies, waits for them, and re-layouts  67.1 us (9%)
  starting transfers between devices  58.9 us (8%)
  other arithmetic  38.3 us (5%)
  between operations  15.7 us (2%)
    all_to_all x4, blocking collectives, to_heads(): traded = lax.all_to_all(item, 'seq', 0, 0)  62.7 us
    all_gather x1, waiting for transfers between devices, local(): down_weight = lax.all_gather(w_down[0], 'fsdp', axis=0, tiled=True)  58.8 us
    reduce_scatter x4, waiting for transfers between devices, over_shards(): return lax.psum_scatter(part, 'fsdp', scatter_dimension=0, tiled=True)  49.6 us
    all_to_all x3, waiting for transfers between devices, over_tokens(): terms = lax.all_to_all(cut_up, 'seq', 0, 0).astype(jnp.float32)  45.8 us
    all_gather x1, waiting for transfers between devices, local(): up_weight = lax.all_gather(w_up[0], 'fsdp', axis=0, tiled=True)  45.8 us
    all_to_all x3, waiting for transfers between devices, over_tokens(): lax.all_to_all(jnp.broadcast_to(own[None], cut_up.shape), 'seq', 0, 0)  41.2 us
    all_to_all x3, waiting for transfers between devices, to_tokens(): return lax.all_to_all(item.reshape(groups, rows, span), 'seq', 0, 0)  37.1 us
    dot_general x19, matrix products, dots(): return jnp.einsum(pattern, left, right, preferred_element_type=jnp.float32)  33.6 us
  transfers between devices with their start and end apart: 23, of which 15 were waited for; matrix products, arithmetic and copies ran while one was open for 9% of the time, Pallas kernels for 0%

profile of v2, /device:TPU:0, one launch (start us, length us, event | category | flops | bytes accessed | tf_op | source)
XLA Modules:
  0.0 739.8 jit_solution(16686354580874201621)
XLA Ops:
  16.6 9.5 %all-gather.4 = s32[4,2,2]{2,1,0:T(2,128)S(1)} all-gather(s32[1,2,2]{2,1,0:T(2,128)S(1)} %bitcast.396), channel_id=1, replica_groups=mesh['pipe'=2,'seq'=4,'fsdp'=4] {'fsdp'}, dimensions={0}, use_global_device_ids=true | all-gather | bytes 80 | tf_op jit(solution)/shard_map/all_gather | solution.py:111
  32.9 8.8 %all-gather.5 = bf16[4,1,2688]{2,1,0:T(2,128)(2,1)S(1)} all-gather(bf16[1,1,2688]{2,1,0:T(2,128)(2,1)S(1)} %reshape.520), channel_id=2, replica_groups=mesh['pipe'=2,'seq'=4,'fsdp'=4] {'fsdp'}, dimensions={0}, use_global_device_ids=true | all-gather | bytes 26880 | tf_op jit(solution)/shard_map/all_gather | solution.py:113
  42.8 27.3 %all-gather.11.cloned.1.call-done = bf16[4,768,576]{2,1,0:T(8,128)(2,1)} async-done(((bf16[4,192,576]{2,1,0:T(8,128)(2,1)}), bf16[4,768,576]{2,1,0:T(8,128)(2,1)}) %all-gather.11.cloned.1.call-update) | async-done | bytes 3538960 | tf_op jit(solution)/shard_map/all_gather | solution.py:124
  73.8 20.3 %all_to_all.103 = bf16[4,128,576]{1,2,0:T(8,128)(2,1)S(1)} all-to-all(bf16[4,128,576]{1,2,0:T(8,128)(2,1)S(1)} %fusion.55), channel_id=1, replica_groups=mesh['pipe'=2,'seq'=4,'fsdp'=4] {'seq'}, dimensions={0} | all-to-all | bytes 1179648 | tf_op jit(solution)/shard_map/all_to_all | solution.py:146
  103.6 6.9 all-to-all-done.2
  112.9 45.8 %all-gather.15.cloned.1.call-done = bf16[1,768,3072]{2,1,0:T(8,128)(2,1)} async-done(((bf16[1,192,3072]{2,1,0:T(8,128)(2,1)}), bf16[1,768,3072]{2,1,0:T(8,128)(2,1)}) %all-gather.15.cloned.1.call-update) | async-done | bytes 4718608 | tf_op jit(solution)/shard_map/all_gather | solution.py:128
  158.7 58.8 %all-gather.17.cloned.1.call-done = bf16[1,3072,768]{2,1,0:T(8,128)(2,1)} async-done(((bf16[1,768,768]{2,1,0:T(8,128)(2,1)}), bf16[1,3072,768]{2,1,0:T(8,128)(2,1)}) %all-gather.17.cloned.1.call-update) | async-done | bytes 4718608 | tf_op jit(solution)/shard_map/all_gather | solution.py:129
  231.0 20.8 %all_to_all.104 = bf16[4,128,576]{1,2,0:T(8,128)(2,1)S(1)} all-to-all(bf16[4,128,576]{1,2,0:T(8,128)(2,1)S(1)} %fusion.54), channel_id=1, replica_groups=mesh['pipe'=2,'seq'=4,'fsdp'=4] {'seq'}, dimensions={0} | all-to-all | bytes 1179648 | tf_op jit(solution)/shard_map/all_to_all | solution.py:146
  263.5 10.0 %all_to_all.105 = bf16[4,128,192]{1,2,0:T(8,128)(2,1)S(1)} all-to-all(bf16[4,128,192]{1,2,0:T(8,128)(2,1)S(1)} %copy.266), channel_id=1, replica_groups=mesh['pipe'=2,'seq'=4,'fsdp'=4] {'seq'}, dimensions={0} | all-to-all | bytes 393216 | tf_op jit(solution)/shard_map/all_to_all | solution.py:154
  281.1 8.7 %fusion.113 = (f32[128]{0:T(128)}, f32[128,768]{1,0:T(8,128)}) fusion(f32[2,768]{1,0:T(2,128)S(1)} %get-tuple-element.56, bf16[1,768,3072]{2,1,0:T(8,128)(2,1)} %all-gather.15.cloned.1.call-done, f32[128,3072]{1,0:T(8,128)} %fusion.21, bf16[128,768]{1,0:T(8,128)(2,1)} %bitcast.376, bf16[1,3072,768]{2,1,0:T(8,128)(2,1)} %all-gather.17.cloned.1.call-done), kind=kOutput, calls=%fused_computation.151 | convolution fusion | flops 1216020352 | bytes 11606528 | tf_op jit(solution)/shard_map/dot_general | solution.py:22
  295.3 9.9 %all_to_all.106 = bf16[4,128,192]{1,2,0:T(8,128)(2,1)} all-to-all(bf16[4,128,192]{1,2,0:T(8,128)(2,1)S(1)} %fusion.72), channel_id=1, replica_groups=mesh['pipe'=2,'seq'=4,'fsdp'=4] {'seq'}, dimensions={0} | all-to-all | bytes 393216 | tf_op jit(solution)/shard_map/all_to_all | solution.py:146
  334.5 13.9 %all-to-all-done.6 = bf16[4,128,576]{1,2,0:T(8,128)(2,1)} async-done(((bf16[4,128,576]{1,2,0:T(8,128)(2,1)}), bf16[4,128,576]{1,2,0:T(8,128)(2,1)}, u32[]{:S(2)}, u32[]{:S(2)}) %all-to-all-start.6) | async-done | bytes 589856 | tf_op jit(solution)/shard_map/all_to_all | solution.py:154
  357.6 10.1 %collective-permute-start.1 = (bf16[2,64,768]{2,1,0:T(8,128)(2,1)S(1)}, bf16[2,64,768]{2,1,0:T(8,128)(2,1)S(1)}, u32[]{:S(2)}, u32[]{:S(2)}) collective-permute-start(bf16[2,64,768]{2,1,0:T(8,128)(2,1)S(1)} %fusion.98), channel_id=1, source_target_pairs={{16,0},{17,1},{18,2},{19,3},{20,4},{21,5},{22,6},{23,7},{24,8},{25... | collective-permute-start | bytes 589832 | tf_op jit(solution)/shard_map/ppermute | solution.py:12
  402.4 11.7 %all_to_all.107 = bf16[4,128,192]{1,2,0:T(8,128)(2,1)} all-to-all(bf16[4,128,192]{1,2,0:T(8,128)(2,1)S(1)} %fusion.73), channel_id=1, replica_groups=mesh['pipe'=2,'seq'=4,'fsdp'=4] {'seq'}, dimensions={0} | all-to-all | bytes 393216 | tf_op jit(solution)/shard_map/all_to_all | solution.py:146
  438.4 16.3 %all-to-all-done.8 = bf16[4,128,576]{1,2,0:T(8,128)(2,1)S(1)} async-done(((bf16[4,128,576]{1,2,0:T(8,128)(2,1)}), bf16[4,128,576]{1,2,0:T(8,128)(2,1)S(1)}, u32[]{:S(2)}, u32[]{:S(2)}) %all-to-all-start.8) | async-done | bytes 589856 | tf_op jit(solution)/shard_map/all_to_all | solution.py:154
  458.9 29.1 %reduce-scatter.5.cloned.1.call-done = bf16[768,768]{1,0:T(8,128)(2,1)} async-done(((bf16[3072,768]{1,0:T(8,128)(2,1)}), bf16[768,768]{1,0:T(8,128)(2,1)}) %reduce-scatter.5.cloned.1.call-update) | async-done | bytes 1179664 | tf_op jit(solution)/shard_map/reduce_scatter | solution.py:193
  504.3 7.5 %all-to-all-done.9 = f32[4,1,15360]{2,1,0:T(1,128)S(1)} async-done(((f32[4,1,15360]{2,1,0:T(1,128)}), f32[4,1,15360]{2,1,0:T(1,128)S(1)}, u32[]{:S(2)}, u32[]{:S(2)}) %all-to-all-start.9) | async-done | bytes 245792 | tf_op jit(solution)/shard_map/all_to_all | solution.py:268
  527.6 20.5 %reduce-scatter.11.cloned.1.call-done = bf16[192,3072]{1,0:T(8,128)(2,1)} async-done(((bf16[768,3072]{1,0:T(8,128)(2,1)}), bf16[192,3072]{1,0:T(8,128)(2,1)}) %reduce-scatter.11.cloned.1.call-update) | async-done | bytes 1179664 | tf_op jit(solution)/shard_map/reduce_scatter | solution.py:193
  548.1 33.2 %all_to_all.108 = bf16[4,48,3072]{2,1,0:T(8,128)(2,1)} all-to-all(bf16[4,48,3072]{2,1,0:T(8,128)(2,1)} %bitcast.368), channel_id=1, replica_groups=mesh['pipe'=2,'seq'=4,'fsdp'=4] {'seq'}, dimensions={0} | all-to-all | bytes 2359296 | tf_op jit(solution)/shard_map/all_to_all | solution.py:249
  586.5 26.0 %all-to-all-done.17 = bf16[4,192,768]{2,1,0:T(8,128)(2,1)S(1)} async-done(((bf16[4,192,768]{2,1,0:T(8,128)(2,1)}), bf16[4,192,768]{2,1,0:T(8,128)(2,1)S(1)}, u32[]{:S(2)}, u32[]{:S(2)}) %all-to-all-start.17) | async-done | bytes 1179680 | tf_op jit(solution)/shard_map/all_to_all | solution.py:249
  613.6 30.5 %all_to_all.109 = bf16[4,48,3072]{2,1,0:T(8,128)(2,1)S(1)} all-to-all(bf16[4,48,3072]{2,1,0:T(8,128)(2,1)S(1)} %broadcast_in_dim.38), channel_id=1, replica_groups=mesh['pipe'=2,'seq'=4,'fsdp'=4] {'seq'}, dimensions={0} | all-to-all | bytes 2359296 | tf_op jit(solution)/shard_map/all_to_all | solution.py:251
  649.9 19.8 %all-to-all-done.11 = bf16[4,48,2304]{2,1,0:T(8,128)(2,1)} async-done(((bf16[4,48,2304]{2,1,0:T(8,128)(2,1)}), bf16[4,48,2304]{2,1,0:T(8,128)(2,1)}, u32[]{:S(2)}, u32[]{:S(2)}) %all-to-all-start.11) | async-done | bytes 884768 | tf_op jit(solution)/shard_map/all_to_all | solution.py:249
  683.2 20.1 %all-to-all-done.18 = bf16[4,192,768]{2,1,0:T(8,128)(2,1)} async-done(((bf16[4,192,768]{2,1,0:T(8,128)(2,1)}), bf16[4,192,768]{2,1,0:T(8,128)(2,1)}, u32[]{:S(2)}, u32[]{:S(2)}) %all-to-all-start.18) | async-done | bytes 1179680 | tf_op jit(solution)/shard_map/all_to_all | solution.py:251
  716.0 14.3 %all-to-all-done.12 = bf16[4,48,2304]{2,1,0:T(8,128)(2,1)} async-done(((bf16[4,48,2304]{2,1,0:T(8,128)(2,1)}), bf16[4,48,2304]{2,1,0:T(8,128)(2,1)}, u32[]{:S(2)}, u32[]{:S(2)}) %all-to-all-start.12) | async-done | bytes 884768 | tf_op jit(solution)/shard_map/all_to_all | solution.py:251
  (399 shorter events, 244.1 us)
Async XLA Ops:
  7.2 62.9 %all-gather.11.cloned.1.call-start = ((), (), s32[]{:S(2)}) async-start(), calls=%async_computation.23 | async-start | bytes 4915200 | tf_op jit(solution)/shard_map/all_gather | solution.py:124
  14.9 88.6 %all-gather.13.cloned.1.call-start = ((), (), s32[]{:S(2)}) async-start(), calls=%async_computation.28 | async-start | bytes 1474560 | tf_op jit(solution)/shard_map/all_gather | solution.py:127
  15.7 143.0 %all-gather.15.cloned.1.call-start = ((), (), s32[]{:S(2)}) async-start(), calls=%async_computation.29 | async-start | bytes 5898240 | tf_op jit(solution)/shard_map/all_gather | solution.py:128
  28.7 13.8 %all-to-all-start = ((f32[4,2,4608]{2,1,0:T(2,128)}), f32[4,2,4608]{2,1,0:T(2,128)S(1)}, u32[]{:S(2)}, u32[]{:S(2)}) async-start(f32[4,2,4608]{2,1,0:T(2,128)} %fusion.24), calls=%async_computation | async-start | bytes 294912 | tf_op jit(solution)/shard_map/all_to_all | solution.py:140
  32.0 185.4 %all-gather.17.cloned.1.call-start = ((), (), s32[]{:S(2)}) async-start(), calls=%async_computation.30 | async-start | bytes 5898240 | tf_op jit(solution)/shard_map/all_gather | solution.py:129
  42.6 180.4 %copy-start.35 = (f32[2,768]{1,0:T(2,128)}, f32[2,768]{1,0:T(2,128)S(1)}, u32[]{:S(2)}) copy-start(f32[2,768]{1,0:T(2,128)S(1)} %get-tuple-element.59) | copy-start | bytes 18436
  99.8 10.6 %all-to-all-start.2 = ((bf16[4,128,192]{1,2,0:T(8,128)(2,1)}), bf16[4,128,192]{1,2,0:T(8,128)(2,1)S(1)}, u32[]{:S(2)}, u32[]{:S(2)}) async-start(bf16[4,128,192]{1,2,0:T(8,128)(2,1)} %copy.258), calls=%async_computation.2 | async-start | bytes 393216 | tf_op jit(solution)/shard_map/all_to_all | solution.py:154
  223.9 2.8 collective-permute-start
  330.3 18.2 %all-to-all-start.6 = ((bf16[4,128,576]{1,2,0:T(8,128)(2,1)}), bf16[4,128,576]{1,2,0:T(8,128)(2,1)}, u32[]{:S(2)}, u32[]{:S(2)}) async-start(bf16[4,128,576]{1,2,0:T(8,128)(2,1)} %copy.273), calls=%async_computation.6 | async-start | bytes 1179648 | tf_op jit(solution)/shard_map/all_to_all | solution.py:154
  334.5 120.3 %reduce-scatter.9.cloned.1.call-start = ((), (), s32[]{:S(2)}) async-start(), calls=%async_computation.26 | async-start | bytes 1474560 | tf_op jit(solution)/shard_map/reduce_scatter | solution.py:193
  357.6 13.6 %collective-permute-start.1 = (bf16[2,64,768]{2,1,0:T(8,128)(2,1)S(1)}, bf16[2,64,768]{2,1,0:T(8,128)(2,1)S(1)}, u32[]{:S(2)}, u32[]{:S(2)}) collective-permute-start(bf16[2,64,768]{2,1,0:T(8,128)(2,1)S(1)} %fusion.98), channel_id=1, source_target_pairs={{16,0},{17,1},{18,2},{19,3},{20,4},{21,5},{22,6},{23,7},{24,8},{25... | collective-permute-start | bytes 589832 | tf_op jit(solution)/shard_map/ppermute | solution.py:12
  400.4 87.6 %reduce-scatter.5.cloned.1.call-start = ((), (), s32[]{:S(2)}) async-start(), calls=%async_computation.24 | async-start | bytes 5898240 | tf_op jit(solution)/shard_map/reduce_scatter | solution.py:193
  401.0 147.1 %reduce-scatter.11.cloned.1.call-start = ((), (), s32[]{:S(2)}) async-start(), calls=%async_computation.27 | async-start | bytes 5898240 | tf_op jit(solution)/shard_map/reduce_scatter | solution.py:193
  434.5 20.2 %all-to-all-start.8 = ((bf16[4,128,576]{1,2,0:T(8,128)(2,1)}), bf16[4,128,576]{1,2,0:T(8,128)(2,1)S(1)}, u32[]{:S(2)}, u32[]{:S(2)}) async-start(bf16[4,128,576]{1,2,0:T(8,128)(2,1)} %copy.280), calls=%async_computation.8 | async-start | bytes 1179648 | tf_op jit(solution)/shard_map/all_to_all | solution.py:154
  454.7 43.2 %all-to-all-start.13 = ((bf16[4,48,768]{2,1,0:T(8,128)(2,1)}), bf16[4,48,768]{2,1,0:T(8,128)(2,1)}, u32[]{:S(2)}, u32[]{:S(2)}) async-start(bf16[4,48,768]{2,1,0:T(8,128)(2,1)} %bitcast.382), calls=%async_computation.16 | async-start | bytes 589824 | tf_op jit(solution)/shard_map/all_to_all | solution.py:249
  458.8 185.4 %reduce-scatter.7.cloned.1.call-start = ((), (), s32[]{:S(2)}) async-start(), calls=%async_computation.25 | async-start | bytes 4423680 | tf_op jit(solution)/shard_map/reduce_scatter | solution.py:193
  498.7 13.1 %all-to-all-start.9 = ((f32[4,1,15360]{2,1,0:T(1,128)}), f32[4,1,15360]{2,1,0:T(1,128)S(1)}, u32[]{:S(2)}, u32[]{:S(2)}) async-start(f32[4,1,15360]{2,1,0:T(1,128)} %broadcast_in_dim.30), calls=%async_computation.10 | async-start | bytes 491520 | tf_op jit(solution)/shard_map/all_to_all | solution.py:268
  512.6 11.7 %all-to-all-start.14 = ((bf16[4,48,768]{2,1,0:T(8,128)(2,1)}), bf16[4,48,768]{2,1,0:T(8,128)(2,1)S(1)}, u32[]{:S(2)}, u32[]{:S(2)}) async-start(bf16[4,48,768]{2,1,0:T(8,128)(2,1)} %broadcast_in_dim.36), calls=%async_computation.17 | async-start | bytes 589824 | tf_op jit(solution)/shard_map/all_to_all | solution.py:251
  524.3 23.9 %all-to-all-start.10 = ((f32[4,1,10752]{2,1,0:T(1,128)}), f32[4,1,10752]{2,1,0:T(1,128)S(1)}, u32[]{:S(2)}, u32[]{:S(2)}) async-start(f32[4,1,10752]{2,1,0:T(1,128)} %all_to_all.73), calls=%async_computation.11 | async-start | bytes 344064 | tf_op jit(solution)/shard_map/all_to_all | solution.py:276
  581.3 31.1 %all-to-all-start.17 = ((bf16[4,192,768]{2,1,0:T(8,128)(2,1)}), bf16[4,192,768]{2,1,0:T(8,128)(2,1)S(1)}, u32[]{:S(2)}, u32[]{:S(2)}) async-start(bf16[4,192,768]{2,1,0:T(8,128)(2,1)} %bitcast.367), calls=%async_computation.21 | async-start | bytes 2359296 | tf_op jit(solution)/shard_map/all_to_all | solution.py:249
  644.2 25.6 %all-to-all-start.11 = ((bf16[4,48,2304]{2,1,0:T(8,128)(2,1)}), bf16[4,48,2304]{2,1,0:T(8,128)(2,1)}, u32[]{:S(2)}, u32[]{:S(2)}) async-start(bf16[4,48,2304]{2,1,0:T(8,128)(2,1)} %bitcast.373), calls=%async_computation.13 | async-start | bytes 1769472 | tf_op jit(solution)/shard_map/all_to_all | solution.py:249
  670.8 32.5 %all-to-all-start.18 = ((bf16[4,192,768]{2,1,0:T(8,128)(2,1)}), bf16[4,192,768]{2,1,0:T(8,128)(2,1)}, u32[]{:S(2)}, u32[]{:S(2)}) async-start(bf16[4,192,768]{2,1,0:T(8,128)(2,1)} %broadcast_in_dim.40), calls=%async_computation.22 | async-start | bytes 2359296 | tf_op jit(solution)/shard_map/all_to_all | solution.py:251
  676.7 31.8 %collective-permute-start.2 = (f32[8,192]{1,0:T(8,128)S(1)}, f32[8,192]{1,0:T(8,128)S(1)}, u32[]{:S(2)}, u32[]{:S(2)}) collective-permute-start(f32[8,192]{1,0:T(8,128)S(1)} %fusion.26), channel_id=1, source_target_pairs={{0,16},{16,0},{1,17},{17,1},{2,18},{18,2},{3,19},{19,3},{4,20},{20... | collective-permute-start | bytes 18440 | tf_op jit(solution)/shard_map/ppermute | solution.py:288
  704.3 26.0 %all-to-all-start.12 = ((bf16[4,48,2304]{2,1,0:T(8,128)(2,1)}), bf16[4,48,2304]{2,1,0:T(8,128)(2,1)}, u32[]{:S(2)}, u32[]{:S(2)}) async-start(bf16[4,48,2304]{2,1,0:T(8,128)(2,1)} %broadcast_in_dim.34), calls=%async_computation.14 | async-start | bytes 1769472 | tf_op jit(solution)/shard_map/all_to_all | solution.py:251
  (75 other events, 894.2 us)
Sparse Core Ops, SparseCore 0:
  15.1 55.0 all-gather.10
  72.0 27.7 all-gather.12
  101.6 57.0 all-gather.14
  160.4 57.0 all-gather.16
  400.5 27.4 reduce-scatter.8
  430.8 57.0 reduce-scatter.4
  491.0 57.0 reduce-scatter.10
  551.8 47.2 reduce-scatter.6
